TPU v7x, 512 devices: a whole 4x4x16 slice. The times are simulated.
512 devices in a mesh: dom: 64 (over z, y), feat: 8 (over x, core).
Axes of the slice: x: 4, y: 4, z: 16, core: 2. Of those that a mesh axis runs over, the one named last changes fastest.
Arguments:
- features: bfloat16 [65536, 1024], P('dom', 'feat'), may hold values from -6 to 6
- history: bfloat16 [65536, 1024], P('dom', 'feat'), may hold values from -6 to 6
- w_root: bfloat16 [1024, 1024], P(None, 'feat'), may hold values from -0.1875 to 0.1875
- w_neigh: bfloat16 [1024, 1024], P(None, 'feat'), may hold values from -0.1875 to 0.1875
- bias: bfloat16 [1024], P('feat'), may hold values from -3 to 3
- local_tiles: bfloat16 [512, 128, 128], P('dom'), may hold values from -0.25 to 0.25
- halo_tiles: bfloat16 [512, 3, 128, 128], P('dom'), may hold values from -0.25 to 0.25
- local_src: int32 [512], P('dom'), may hold values from 0 to 7
- halo_src: int32 [512, 3], P('dom'), may hold values from 0 to 63
- halo_count: int32 [512], P('dom'), may hold values from 1 to 3
- halo_peer: int32 [4096, 1], P('dom'), may hold values from 0 to 62; in each aligned block of 64 rows (0 to 63, 64 to 127, ...) at most 2 rows name the same one
- halo_block: int32 [4096], P('dom'), may hold values from 0 to 7
Outputs:
- output: bfloat16 [65536, 1024], P('dom', 'feat')
Inputs may be any that keep to these rules, and one draw needn't show every extreme that they name: `halo_peer`: among the 64 slots of one partition no offset appears more than 2 times, and some offset appears exactly 2 times; offset r names partition (p + 1 + r) mod 64, never p itself. Halo tiles j >= halo_count[b] of a target block are unused.
All inputs are finite; a program needn't handle non-finite values.
Results may differ from a plain program's by a relative error of at most 0.0037.
Values may be sent and summed in bfloat16 or wider, within the bound.
No kernel may reach another device: no remote copies, remote signals or barrier semaphores. Data moves between devices by JAX's collectives and lax.ppermute only.
A program may use at most 64 MiB of HBM per device.

v0:
```python
import jax
import jax.numpy as jnp
from jax import lax
from jax.sharding import PartitionSpec as P

CAP = 2


def body(
    features,
    history,
    w_root,
    w_neigh,
    bias,
    local_tiles,
    halo_tiles,
    local_src,
    halo_src,
    halo_count,
    halo_peer,
    halo_block,
):
    row_count, columns = features.shape
    block_rows = local_tiles.shape[1]
    block_count = row_count // block_rows
    partitions = lax.axis_size("dom")
    my_index = lax.axis_index("dom")
    halo_slots = halo_block.shape[0]
    owners = (my_index + 1 + halo_peer[:, 0]) % partitions
    same_owner = owners[:, None] == owners[None, :]
    earlier = lax.broadcasted_iota(jnp.int32, (halo_slots, halo_slots), 1) < lax.broadcasted_iota(
        jnp.int32, (halo_slots, halo_slots), 0
    )
    rank_of = jnp.sum(jnp.logical_and(same_owner, earlier).astype(jnp.int32), axis=1)
    placed = owners * CAP + rank_of
    slot_hits = placed[:, None] == jnp.arange(partitions * CAP, dtype=jnp.int32)[None, :]
    wanted_ids = jnp.sum(jnp.where(slot_hits, halo_block[:, None], 0), axis=0)
    requests = jnp.where(jnp.any(slot_hits, axis=0), wanted_ids, -1).reshape(partitions, CAP)
    stored = history.reshape(-1, block_rows, columns)
    wanted = lax.all_to_all(requests, "dom", split_axis=0, concat_axis=0, tiled=True)
    wanted_ok = wanted >= 0
    picked = stored[jnp.clip(wanted, 0, stored.shape[0] - 1)]
    picked = jnp.where(wanted_ok[:, :, None, None], picked, jnp.zeros((), picked.dtype))
    arrived = lax.all_to_all(picked, "dom", split_axis=0, concat_axis=0, tiled=True)
    own_blocks = features.reshape(block_count, block_rows, columns)
    local_part = jnp.einsum(
        "bij,bjc->bic", local_tiles, own_blocks[local_src], preferred_element_type=jnp.float32
    )
    halo_rows = arrived.reshape(-1, block_rows, columns)[placed]
    active = lax.broadcasted_iota(jnp.int32, halo_src.shape, 1) < halo_count[:, None]
    masked = jnp.where(active[:, :, None, None], halo_tiles, jnp.zeros((), halo_tiles.dtype))
    halo_part = jnp.einsum(
        "bkij,bkjc->bic", masked, halo_rows[halo_src], preferred_element_type=jnp.float32
    )
    aggregate = (local_part + halo_part).astype(jnp.bfloat16).reshape(row_count, columns)
    running = jnp.dot(
        lax.all_gather(features, "feat", axis=1, tiled=True),
        w_root,
        preferred_element_type=jnp.float32,
    )
    mixed = running + jnp.dot(
        lax.all_gather(aggregate, "feat", axis=1, tiled=True),
        w_neigh,
        preferred_element_type=jnp.float32,
    )
    return jax.nn.relu(mixed + bias.astype(jnp.float32)).astype(jnp.bfloat16)


def solution(mesh):
    in_specs = (
        P("dom", "feat"),
        P("dom", "feat"),
        P(None, "feat"),
        P(None, "feat"),
        P("feat"),
        P("dom", None, None),
        P("dom", None, None, None),
        P("dom"),
        P("dom", None),
        P("dom"),
        P("dom", None),
        P("dom"),
    )
    out_specs = P("dom", "feat")
    return jax.shard_map(body, mesh=mesh, in_specs=in_specs, out_specs=out_specs, check_vma=False)
```

profile of v0, /device:TPU:1, one launch (start us, length us, event | category | flops | bytes accessed | tf_op | source)
XLA Modules:
  0.0 289.7 jit_solution(9422044633904263521)
XLA Ops:
  6.5 0.7 and_select_fusion
  7.2 0.7 fusion.23
  7.9 0.2 convert_reduce_fusion
  8.1 0.7 fusion.12
  8.8 0.1 fusion.8
  8.9 0.8 select_reduce_fusion
  9.6 0.1 select_n.69
  9.8 32.5 %all_to_all.11 = s32[64,1,2]{2,1,0:T(1,128)S(1)} all-to-all(s32[64,1,2]{2,1,0:T(1,128)S(1)} %bitcast.48), channel_id=1, replica_groups=mesh['dom'=64,'feat'=8] {'dom'}, dimensions={0} | all-to-all | bytes 1024 | tf_op jit(solution)/shard_map/all_to_all | solution.py:40
  42.3 0.1 copy.36
  42.4 0.1 copy.39
  42.5 0.1 reshape.120
  42.6 0.1 copy.37
  42.8 3.1 %gather_fusion.1 = bf16[128,128,128]{2,1,0:T(8,128)(2,1)} fusion(bf16[8,128,128]{2,1,0:T(8,128)(2,1)S(1)} %bitcast.43, s32[1024]{0:T(1024)S(1)} %pad_clamp_fusion.2), kind=kCustom, calls=%fused_computation.1 | custom fusion | bytes 8389120 | tf_op jit(solution)/shard_map/gather | solution.py:42
  45.8 4.5 %broadcast_select_fusion = bf16[64,2,128,128]{3,2,1,0:T(8,128)(2,1)} fusion(bf16[64,2,128,128]{3,2,1,0:T(8,128)(2,1)} %bitcast.44, pred[64,2]{1,0:T(8,128)(4,1)S(1)} %copy.37), kind=kLoop, calls=%fused_computation.4 | loop fusion | flops 2097152 | bytes 8388736 | tf_op jit(solution)/shard_map/jit(_where)/select_n | solution.py:43
  50.3 5.8 %all-to-all-start.1 = ((bf16[64,2,128,128]{3,2,1,0:T(8,128)(2,1)}), bf16[64,2,128,128]{3,2,1,0:T(8,128)(2,1)}, u32[]{:S(2)}, u32[]{:S(2)}) async-start(bf16[64,2,128,128]{3,2,1,0:T(8,128)(2,1)} %broadcast_select_fusion), calls=%async_computation.1 | async-start | bytes 8388608 | tf_op jit(solution)/shard_map/all_to_all | solution.py:44
  56.1 0.0 all-gather.3.cloned.1.call-start
  56.2 0.7 all-gather.3.cloned.1.call-update
  56.9 0.0 all-gather.5.cloned.1.call-start
  56.9 0.1 copy.40
  57.0 0.1 reshape.136
  57.1 0.6 gather_fusion
  57.8 0.1 iota_compare_fusion.2
  57.9 180.8 %all-to-all-done.1 = bf16[64,2,128,128]{3,2,1,0:T(8,128)(2,1)} async-done(((bf16[64,2,128,128]{3,2,1,0:T(8,128)(2,1)}), bf16[64,2,128,128]{3,2,1,0:T(8,128)(2,1)}, u32[]{:S(2)}, u32[]{:S(2)}) %all-to-all-start.1) | async-done | bytes 4194336 | tf_op jit(solution)/shard_map/all_to_all | solution.py:44
  238.7 3.1 %gather_fusion.2 = bf16[64,128,128]{2,1,0:T(8,128)(2,1)S(1)} fusion(bf16[128,128,128]{2,1,0:T(8,128)(2,1)} %bitcast.11, s32[1024]{0:T(1024)S(1)} %pad_clamp_fusion.1), kind=kCustom, calls=%fused_computation.2 | custom fusion | bytes 4194560 | tf_op jit(solution)/shard_map/gather | solution.py:49
  241.8 0.7 gather_fusion.3
  242.6 1.6 convolution_bitcast_fusion.1
  244.2 0.9 fusion.4
  245.1 0.0 all-gather.5.cloned.1.call-update
  245.2 0.0 all-gather.3.cloned.1.call-done
  245.2 2.3 fusion.15
  247.5 32.4 %all-gather.5.cloned.1.call-done = bf16[1024,1024]{1,0:T(8,128)(2,1)} async-done(((bf16[1024,128]{1,0:T(8,128)(2,1)}), bf16[1024,1024]{1,0:T(8,128)(2,1)}) %all-gather.5.cloned.1.call-update) | async-done | bytes 2097168 | tf_op jit(solution)/shard_map/all_gather | solution.py:62
  279.9 3.0 %fusion.3 = bf16[1024,128]{1,0:T(8,128)(2,1)} fusion(f32[1024,128]{1,0:T(8,128)S(1)} %fusion.15, bf16[1024,1024]{1,0:T(8,128)(2,1)} %all-gather.5.cloned.1.call-done, bf16[1024,128]{1,0:T(8,128)(2,1)S(1)} %copy-done.4, f32[128]{0:T(128)S(1)} %convert_element_type.14), kind=kOutput, calls=%fused_computation.11 | convolution fusion | flops 268959744 | bytes 3146240 | tf_op jit(solution)/shard_map/dot_general | solution.py:61
  (28 shorter events, 0.1 us)
Async XLA Ops:
  6.5 36.2 %copy-start = (bf16[1024,128]{1,0:T(8,128)(2,1)S(1)}, bf16[1024,128]{1,0:T(8,128)(2,1)}, u32[]{:S(2)}) copy-start(bf16[1024,128]{1,0:T(8,128)(2,1)} %param.13) | copy-start | bytes 786436
  50.3 6.6 %copy-start.5 = (s32[8,3]{0,1:T(4,128)S(1)}, s32[8,3]{0,1:T(4,128)}, u32[]{:S(2)}) copy-start(s32[8,3]{0,1:T(4,128)} %param.20) | copy-start | bytes 292
  50.3 6.8 %copy-start.6 = (s32[8]{0:T(128)S(1)}, s32[8]{0:T(128)}, u32[]{:S(2)}) copy-start(s32[8]{0:T(128)} %param.19) | copy-start | bytes 100
  50.3 6.8 %copy-start.1 = (bf16[1024,128]{1,0:T(8,128)(2,1)S(1)}, bf16[1024,128]{1,0:T(8,128)(2,1)}, u32[]{:S(2)}) copy-start(bf16[1024,128]{1,0:T(8,128)(2,1)} %param.12) | copy-start | bytes 786436
  50.3 7.4 %copy-start.7 = (s32[8]{0:T(128)S(1)}, s32[8]{0:T(128)}, u32[]{:S(2)}) copy-start(s32[8]{0:T(128)} %param.21) | copy-start | bytes 100
  50.3 188.3 %all-to-all-start.1 = ((bf16[64,2,128,128]{3,2,1,0:T(8,128)(2,1)}), bf16[64,2,128,128]{3,2,1,0:T(8,128)(2,1)}, u32[]{:S(2)}, u32[]{:S(2)}) async-start(bf16[64,2,128,128]{3,2,1,0:T(8,128)(2,1)} %broadcast_select_fusion), calls=%async_computation.1 | async-start | bytes 8388608 | tf_op jit(solution)/shard_map/all_to_all | solution.py:44
  56.1 189.1 %all-gather.3.cloned.1.call-start = ((), (), s32[]{:S(2)}) async-start(), calls=%async_computation.2 | async-start | bytes 2359296 | tf_op jit(solution)/shard_map/all_gather | solution.py:57
  56.9 223.0 %all-gather.5.cloned.1.call-start = ((), (), s32[]{:S(2)}) async-start(), calls=%async_computation.3 | async-start | bytes 2359296 | tf_op jit(solution)/shard_map/all_gather | solution.py:62
  242.5 1.6 copy-start.2
  242.5 2.6 copy-start.8
  242.5 2.6 copy-start.3
  244.2 35.7 %copy-start.4 = (bf16[1024,128]{1,0:T(8,128)(2,1)S(1)}, bf16[1024,128]{1,0:T(8,128)(2,1)}, u32[]{:S(2)}) copy-start(bf16[1024,128]{1,0:T(8,128)(2,1)} %param.15) | copy-start | bytes 786436
Sparse Core Ops, SparseCore 0:
  59.1 37.4 all-gather.2
  245.3 34.5 all-gather.4
where the time goes:
time: 290 us
  waiting for transfers between devices  214 us (74%)
  blocking collectives  32.5 us (11%)
  between operations  13.6 us (5%)
  local copies, waits for them, and re-layouts  8.25 us (3%)
  matrix products  7.83 us (3%)
  other arithmetic  7.69 us (3%)
  starting transfers between devices  5.88 us (2%)
    all_to_all x1, waiting for transfers between devices, body(): lax.all_to_all(picked, 'dom', split_axis=0, concat_axis=0, tiled=True)  181 us
    all_to_all x1, blocking collectives, body(): lax.all_to_all(requests, 'dom', split_axis=0, concat_axis=0, tiled=True)  32.5 us
    all_gather x1, waiting for transfers between devices, body(): lax.all_gather(aggregate, 'feat', axis=1, tiled=True)  32.4 us
    all_to_all x1, starting transfers between devices, body(): lax.all_to_all(picked, 'dom', split_axis=0, concat_axis=0, tiled=True)  5.8 us
  transfers between devices with their start and end apart: 3, of which 2 were waited for; matrix products, arithmetic and copies ran while one was open for 3% of the time, Pallas kernels for 0%

commit v1 on v0

v1 whole, which is shorter than its diff:
```python
import jax
import jax.numpy as jnp
from jax import lax
from jax.experimental import pallas as pl
from jax.experimental.pallas import tpu as pltpu
from jax.sharding import Mesh
from jax.sharding import PartitionSpec as P

Z, Y, X, CORE = 16, 4, 4, 2
BLK = 128
TB = 8
HT = 3
REFS = TB * HT
HALF = REFS // CORE
META = 16
GROUP = 4


def pick_kernel(count, slot, core, mine, other, picked, sem):
    def copy(peer, i, tiles):
        row = pl.multiple_of(slot[peer, i] % HALF * BLK, BLK)
        return pltpu.make_async_copy(tiles.at[peer, pl.ds(row, BLK)], picked.at[peer, i], sem.at[peer, i])

    for peer in range(Y):

        @pl.loop(0, count[peer])
        def _(i):
            from_mine = slot[peer, i] // HALF == core[0]

            @pl.when(from_mine)
            def _():
                copy(peer, i, mine).start()

            @pl.when(jnp.logical_not(from_mine))
            def _():
                copy(peer, i, other).start()

    for peer in range(Y):

        @pl.loop(0, count[peer])
        def _(i):
            copy(peer, i, mine).wait()


def partial_kernel(
    count, source, target, me, blocks, tiles, sent, own, block_buf, tile_buf, sent_buf, total, block_sem, tile_sem, out_sem
):
    def groups(peer):
        return (count[peer] + GROUP - 1) // GROUP

    def block_copy(peer, i):
        row = pl.multiple_of(source[peer, i] * BLK, BLK)
        return pltpu.make_async_copy(blocks.at[pl.ds(row, BLK)], block_buf.at[peer, i], block_sem.at[peer, i])

    def tile_copy(peer, group):
        at = pl.ds(group * GROUP, GROUP)
        return pltpu.make_async_copy(tiles.at[peer, at], tile_buf.at[peer, at], tile_sem.at[peer, group])

    for peer in range(Y):

        @pl.loop(0, groups(peer))
        def _(group):
            tile_copy(peer, group).start()
            for u in range(GROUP):
                i = group * GROUP + u

                @pl.when(i < count[peer])
                def _():
                    block_copy(peer, i).start()

    total[...] = jnp.zeros_like(total)
    copies = []
    for peer in range(Y):

        @pl.loop(0, groups(peer))
        def _(group):
            members = [group * GROUP + u for u in range(GROUP)]
            tile_copy(peer, group).wait()
            for i in members:

                @pl.when(i < count[peer])
                def _():
                    block_copy(peer, i).wait()

            products = [
                jnp.dot(tile_buf[peer, i], block_buf[peer, i], preferred_element_type=jnp.float32) for i in members
            ]
            for i, part in zip(members, products):
                total[target[peer, i]] += part

        at = pl.ds(peer * TB, TB)
        sent_buf[at] = jnp.where(me[0] == peer, 0.0, total[at]).astype(sent.dtype)
        copies.append(pltpu.make_async_copy(sent_buf.at[at], sent.at[at], out_sem.at[peer]))
        copies[-1].start()
    copies.append(pltpu.make_async_copy(total.at[pl.ds(me[0] * TB, TB)], own, out_sem.at[Y]))
    copies[-1].start()
    for copy in copies:
        copy.wait()


def partial_sums(place, me, core, blocks, mine, other):
    active = place >= 0
    rank = jnp.cumsum(active.astype(jnp.int32), axis=1) - 1
    numbers = jnp.arange(REFS, dtype=jnp.int32)
    hits = jnp.logical_and(active, rank == numbers[:, None, None])
    count = jnp.sum(active.astype(jnp.int32), axis=1)

    def listed(values, spare):
        return (jnp.sum(jnp.where(hits, values - spare, 0), axis=2) + spare).T

    smem, hbm, vmem = (pl.BlockSpec(memory_space=m) for m in (pltpu.SMEM, pltpu.HBM, pltpu.VMEM))
    picked = pl.pallas_call(
        pick_kernel,
        out_shape=jax.ShapeDtypeStruct((Y, REFS, BLK, BLK), jnp.bfloat16),
        in_specs=[smem] * 3 + [hbm] * 2,
        out_specs=vmem,
        scratch_shapes=[pltpu.SemaphoreType.DMA((Y, REFS))],
        compiler_params=pltpu.CompilerParams(vmem_limit_bytes=8 * 1024 * 1024),
        cost_estimate=pl.CostEstimate(flops=0, bytes_accessed=4 * 2**20, transcendentals=0),
        name="pick_tiles",
    )(count, listed(numbers, 0), core, mine, other)
    return pl.pallas_call(
        partial_kernel,
        out_shape=(
            jax.ShapeDtypeStruct((Y * TB, BLK, BLK), jnp.bfloat16),
            jax.ShapeDtypeStruct((TB, BLK, BLK), jnp.float32),
        ),
        in_specs=[smem] * 4 + [hbm] * 2,
        out_specs=(hbm, hbm),
        scratch_shapes=[
            pltpu.VMEM((Y, REFS, BLK, BLK), jnp.bfloat16),
            pltpu.VMEM((Y, REFS, BLK, BLK), jnp.bfloat16),
            pltpu.VMEM((Y * TB, BLK, BLK), jnp.bfloat16),
            pltpu.VMEM((Y * TB + 1, BLK, BLK), jnp.float32),
            pltpu.SemaphoreType.DMA((Y, REFS)),
            pltpu.SemaphoreType.DMA((Y, REFS // GROUP)),
            pltpu.SemaphoreType.DMA((Y + 1,)),
        ],
        compiler_params=pltpu.CompilerParams(vmem_limit_bytes=60 * 1024 * 1024),
        cost_estimate=pl.CostEstimate(flops=REFS * 2 * BLK**3, bytes_accessed=4 * 2**20, transcendentals=0),
        name="partial_sums",
    )(
        count,
        listed(place, 0),
        listed(numbers // HT + TB * jnp.arange(Y, dtype=jnp.int32)[:, None], Y * TB),
        me,
        blocks,
        picked,
    )


def product_kernel(mine, other, weight, out):
    rows = 256

    @pl.loop(0, out.shape[0] // rows)
    def _(step):
        at = pl.ds(pl.multiple_of(step * rows, rows), rows)
        total = None
        for i in range(X):
            pair = jnp.concatenate([mine[i, at], other[i, at]], axis=1)
            part = jnp.dot(pair, weight[i], preferred_element_type=jnp.float32)
            total = part if total is None else total + part
        out[at] = total.astype(out.dtype)


def product(gathered, weight, dtype):
    mine, other = gathered
    shape = (mine.shape[1], weight.shape[-1])
    vmem = pl.BlockSpec(memory_space=pltpu.VMEM)
    return pl.pallas_call(
        product_kernel,
        out_shape=jax.ShapeDtypeStruct(shape, dtype),
        in_specs=[vmem] * 3,
        out_specs=vmem,
        compiler_params=pltpu.CompilerParams(vmem_limit_bytes=16 * 1024 * 1024),
        cost_estimate=pl.CostEstimate(flops=2 * shape[0] * 1024 * shape[1], bytes_accessed=4 * 2**20, transcendentals=0),
        name="product",
    )(mine, other, weight)


def own_core_first(weight, core):
    parts = weight.reshape(X, CORE, -1, weight.shape[1])
    return jnp.where(core == 0, parts, parts[:, ::-1]).reshape(X, -1, weight.shape[1])


def to_all(array, axis, size):
    return lax.all_to_all(jnp.broadcast_to(array[None], (size,) + array.shape), axis, 0, 0, tiled=True)


def swap_cores(array):
    return lax.ppermute(array, "core", [(0, 1), (1, 0)])


def all_columns(array):
    mine = to_all(array, "x", X)
    return mine, swap_cores(mine)


def body(
    features,
    history,
    w_root,
    w_neigh,
    bias,
    local_tiles,
    halo_tiles,
    local_src,
    halo_src,
    halo_count,
    halo_peer,
    halo_block,
):
    rows, columns = features.shape
    my_z, my_y, my_core = lax.axis_index("z"), lax.axis_index("y"), lax.axis_index("core")

    mixed_history = product(all_columns(history), own_core_first(w_neigh, my_core), jnp.bfloat16)
    column_blocks = lax.all_gather(mixed_history, "z", axis=0, tiled=True)

    _, features, w_neigh, halo_tiles, halo_src, halo_count, halo_peer, halo_block = lax.optimization_barrier(
        (mixed_history, features, w_neigh, halo_tiles, halo_src, halo_count, halo_peer, halo_block)
    )

    owners = (my_z * Y + my_y + 1 + halo_peer[:, 0]) % (Z * Y)
    hits = halo_src.reshape(REFS, 1) == jnp.arange(halo_block.shape[0], dtype=jnp.int32)[None, :]
    used = (lax.broadcasted_iota(jnp.int32, (TB, HT), 1) < halo_count[:, None]).reshape(REFS)
    code = jnp.sum(jnp.where(hits, (owners * TB + halo_block)[None, :], 0), axis=1)
    code = jnp.where(used, code, -TB)
    notes = jnp.stack([code // TB, code % TB])
    notes = jnp.pad(notes, ((0, META - 2), (0, BLK - REFS))).astype(jnp.bfloat16)
    share = lax.dynamic_slice_in_dim(halo_tiles.reshape(REFS * BLK, BLK), my_core * HALF * BLK, HALF * BLK)
    mine = to_all(jnp.concatenate([share, notes]), "y", Y)
    other = swap_cores(mine)
    told = mine[:, HALF * BLK : HALF * BLK + 2, :REFS].astype(jnp.int32)
    owner, block = told[:, 0], told[:, 1]
    here = jnp.logical_and(owner >= 0, owner % Y == my_y)
    place = jnp.where(here, owner // Y * TB + block, -1)

    all_features = all_columns(features)
    own_mixed = product(all_features, own_core_first(w_neigh, my_core), jnp.bfloat16).reshape(TB, BLK, columns)
    local_part = jnp.einsum("bij,bjc->bic", local_tiles, own_mixed[local_src], preferred_element_type=jnp.float32)
    root = product(all_features, own_core_first(w_root, my_core), jnp.float32)
    base = root + local_part.reshape(rows, columns) + bias.astype(jnp.float32)

    sent, own = partial_sums(place, my_y.reshape(1), my_core.reshape(1), column_blocks, mine, other)
    came = lax.all_to_all(sent.reshape(Y, rows, columns), "y", 0, 0, tiled=True)
    total = lax.optimization_barrier(base + own.reshape(rows, columns))
    for i in range(Y):
        total = total + came[i].astype(jnp.float32)
    return jax.nn.relu(total).astype(jnp.bfloat16)


def solution(mesh):
    chips = Mesh(mesh.devices.reshape(Z, Y, X, CORE), ("z", "y", "x", "core"))
    dom, feat = ("z", "y"), ("x", "core")
    in_specs = (
        P(dom, feat),
        P(dom, feat),
        P(None, feat),
        P(None, feat),
        P(feat),
        P(dom, None, None),
        P(dom, None, None, None),
        P(dom),
        P(dom, None),
        P(dom),
        P(dom, None),
        P(dom),
    )
    return jax.shard_map(body, mesh=chips, in_specs=in_specs, out_specs=P(dom, feat), check_vma=False)
```

time: 290 us -> 143 us (0.49)
  the two profiles are of different devices: /device:TPU:1 before, /device:TPU:4 now
where the time goes in v1:
time: 143 us
  waiting for transfers between devices  44.6 us (31%)
  blocking collectives  42.6 us (30%)
  starting transfers between devices  16.3 us (11%)
  Pallas kernels  15 us (10%)
  between operations  13.7 us (10%)
  local copies, waits for them, and re-layouts  5.82 us (4%)
  other arithmetic  4.42 us (3%)
    all_to_all x2, blocking collectives, to_all(): lax.all_to_all(jnp.broadcast_to(array[None], (size,) + array.shape), axis...  42.6 us
    all_gather x1, waiting for transfers between devices, body(): column_blocks = lax.all_gather(mixed_history, 'z', axis=0, tiled=True)  29.3 us
    all_to_all x1, waiting for transfers between devices, to_all(): lax.all_to_all(jnp.broadcast_to(array[None], (size,) + array.shape), axis...  9.58 us
    pallas_call x3, Pallas kernels, product(): pl.pallas_call(product_kernel, out_shape=jax.ShapeDtypeStruct(shape, dtyp...  6.67 us
    all_to_all x1, starting transfers between devices, to_all(): lax.all_to_all(jnp.broadcast_to(array[None], (size,) + array.shape), axis...  6.2 us
    ppermute x3, starting transfers between devices, swap_cores(): return lax.ppermute(array, 'core', [(0, 1), (1, 0)])  5.73 us
    pallas_call x1, Pallas kernels, partial_sums(): pl.pallas_call(partial_kernel, out_shape=(jax.ShapeDtypeStruct((Y * TB, B...  4.83 us
    all_to_all x1, starting transfers between devices, body(): came = lax.all_to_all(sent.reshape(Y, rows, columns), 'y', 0, 0, tiled=True)  4.4 us
  transfers between devices with their start and end apart: 6, of which 4 were waited for; matrix products, arithmetic and copies ran while one was open for 5% of the time, Pallas kernels for 9%

profile of v1, /device:TPU:4, one launch (start us, length us, event | category | flops | bytes accessed | tf_op | source)
XLA Modules:
  0.0 142.7 jit_solution(15982809670616585451)
XLA Ops:
  6.5 1.2 broadcast_in_dim.66
  7.7 17.0 %all_to_all.20.mine = bf16[4,1024,128]{2,1,0:T(8,128)(2,1)S(1)} all-to-all(bf16[4,1024,128]{2,1,0:T(8,128)(2,1)S(1)} %broadcast_in_dim.66), channel_id=1, replica_groups=mesh['z'=16,'y'=4,'x'=4,'core'=2] {'x'}, dimensions={0} | all-to-all | bytes 2097152 | tf_op jit(solution)/shard_map/all_to_all | solution.py:187
  24.7 1.9 %collective-permute-start = (bf16[4,1024,128]{2,1,0:T(8,128)(2,1)S(1)}, bf16[4,1024,128]{2,1,0:T(8,128)(2,1)S(1)}, u32[]{:S(2)}, u32[]{:S(2)}) collective-permute-start(bf16[4,1024,128]{2,1,0:T(8,128)(2,1)S(1)} %all_to_all.20.mine), channel_id=1, source_target_pairs={{0,1},{1,0},{2,3},{3,2},{4,5},{5,4},{6,7},{7,6},{8,9},{9,8},{10,11... | collective-permute-start | bytes 3145736 | tf_op jit(solution)/shard_map/ppermute | solution.py:191
  26.7 2.5 %collective-permute-done.other = bf16[4,1024,128]{2,1,0:T(8,128)(2,1)S(1)} collective-permute-done((bf16[4,1024,128]{2,1,0:T(8,128)(2,1)S(1)}, bf16[4,1024,128]{2,1,0:T(8,128)(2,1)S(1)}, u32[]{:S(2)}, u32[]{:S(2)}) %collective-permute-start) | collective-permute-done | bytes 1048608 | tf_op jit(solution)/shard_map/ppermute | solution.py:191
  29.2 1.8 %product.3 = bf16[1024,128]{1,0:T(8,128)(2,1)} custom-call(bf16[4,1024,128]{2,1,0:T(8,128)(2,1)S(1)} %all_to_all.20.mine, bf16[4,1024,128]{2,1,0:T(8,128)(2,1)S(1)} %collective-permute-done.other, bf16[4,256,128]{2,1,0:T(8,128)(2,1)S(1)} %bitcast.59), custom_call_target="tpu_custom_call" | custom-call | flops 268435456 | bytes 4194304 | tf_op jit(solution)/shard_map/product/pallas_call | solution.py:170
  31.1 0.1 copy.15
  31.2 0.1 eq.54
  31.4 0.1 lt.51
  31.5 0.2 select_reduce_fusion.3
  31.8 0.2 broadcast_in_dim.72
  32.0 25.6 %all_to_all.21.mine = bf16[4,1552,128]{2,1,0:T(8,128)(2,1)S(1)} all-to-all(bf16[4,1552,128]{2,1,0:T(8,128)(2,1)S(1)} %broadcast_in_dim.72), channel_id=1, replica_groups=mesh['z'=16,'y'=4,'x'=4,'core'=2] {'y'}, dimensions={0} | all-to-all | bytes 3178496 | tf_op jit(solution)/shard_map/all_to_all | solution.py:187
  57.6 1.1 broadcast_in_dim.67
  58.7 6.2 %all-to-all-start.1 = ((bf16[4,1024,128]{2,1,0:T(8,128)(2,1)}), bf16[4,1024,128]{2,1,0:T(8,128)(2,1)S(1)}, u32[]{:S(2)}, u32[]{:S(2)}) async-start(bf16[4,1024,128]{2,1,0:T(8,128)(2,1)} %broadcast_in_dim.67), calls=%async_computation.1 | async-start | bytes 2097152 | tf_op jit(solution)/shard_map/all_to_all | solution.py:187
  65.0 1.9 %collective-permute-start.2 = (bf16[4,1552,128]{2,1,0:T(8,128)(2,1)S(1)}, bf16[4,1552,128]{2,1,0:T(8,128)(2,1)}, u32[]{:S(2)}, u32[]{:S(2)}) collective-permute-start(bf16[4,1552,128]{2,1,0:T(8,128)(2,1)S(1)} %all_to_all.21.mine), channel_id=1, source_target_pairs={{0,1},{1,0},{2,3},{3,2},{4,5},{5,4},{6,7},{7,6},{8,9},{9,8},{10,11... | collective-permute-start | bytes 4767752 | tf_op jit(solution)/shard_map/ppermute | solution.py:191
  66.9 9.6 %all-to-all-done.1.mine = bf16[4,1024,128]{2,1,0:T(8,128)(2,1)S(1)} async-done(((bf16[4,1024,128]{2,1,0:T(8,128)(2,1)}), bf16[4,1024,128]{2,1,0:T(8,128)(2,1)S(1)}, u32[]{:S(2)}, u32[]{:S(2)}) %all-to-all-start.1) | async-done | bytes 1048608 | tf_op jit(solution)/shard_map/all_to_all | solution.py:187
  76.5 1.9 %collective-permute-start.1 = (bf16[4,1024,128]{2,1,0:T(8,128)(2,1)S(1)}, bf16[4,1024,128]{2,1,0:T(8,128)(2,1)}, u32[]{:S(2)}, u32[]{:S(2)}) collective-permute-start(bf16[4,1024,128]{2,1,0:T(8,128)(2,1)S(1)} %all-to-all-done.1.mine), channel_id=1, source_target_pairs={{0,1},{1,0},{2,3},{3,2},{4,5},{5,4},{6,7},{7,6},{8,9},{9,8},{10,11... | collective-permute-start | bytes 3145736 | tf_op jit(solution)/shard_map/ppermute | solution.py:191
  78.5 0.2 reduce_window_sum.11
  78.7 0.1 convert_reduce_fusion.count
  78.9 0.9 select_reduce_fusion
  79.8 0.6 add_bitcast_fusion.target
  80.3 3.5 %pick_tiles.1.tiles = bf16[4,24,128,128]{3,2,1,0:T(8,128)(2,1)S(1)} custom-call(s32[4]{0:T(128)S(1)} %convert_reduce_fusion.count, s32[4,24]{1,0:T(4,128)S(1)} %bitcast.63, s32[1]{0:T(128)} %bitcast.18.core, bf16[4,1552,128]{2,1,0:T(8,128)(2,1)S(1)} %all_to_all.21.mine, bf16[4,1552,128]{2,1,0:T(8,128)(2,1)} %collective-permute-done.2.other), custom_call_target="tpu_custom_call" | custom-call | bytes 4194304 | tf_op jit(solution)/shard_map/pick_tiles/pallas_call | solution.py:112
  83.8 1.7 %copy-done.1 = bf16[4,24,128,128]{3,2,1,0:T(8,128)(2,1)} copy-done((bf16[4,24,128,128]{3,2,1,0:T(8,128)(2,1)}, bf16[4,24,128,128]{3,2,1,0:T(8,128)(2,1)S(1)}, u32[]{:S(2)}) %copy-start.1) | copy-done | bytes 3145752
  85.5 29.3 %all-gather.2.cloned.1.call-done.blocks = bf16[16384,128]{1,0:T(8,128)(2,1)} async-done(((bf16[1024,128]{1,0:T(8,128)(2,1)}), bf16[16384,128]{1,0:T(8,128)(2,1)}) %all-gather.2.cloned.1.call-update) | async-done | bytes 4194320 | tf_op jit(solution)/shard_map/all_gather | solution.py:217
  114.8 4.8 %partial_sums.1 = (bf16[32,128,128]{2,1,0:T(8,128)(2,1)}, f32[8,128,128]{2,1,0:T(8,128)}) custom-call(s32[4]{0:T(128)} %copy-done.2, s32[4,24]{1,0:T(4,128)} %bitcast.68, s32[4,24]{1,0:T(4,128)} %add_bitcast_fusion.target, s32[1]{0:T(128)} %bitcast.16.me, bf16[16384,128]{1,0:T(8,128)(2,1)} %all-gather.2.cloned.1.call-done.blocks, ...), custom_call_target="tpu_custom_call" | custom-call | flops 100663296 | bytes 4194304 | tf_op jit(solution)/shard_map/partial_sums/pallas_call | solution.py:122
  119.7 4.4 %all-to-all-start.3 = ((bf16[4,1024,128]{2,1,0:T(8,128)(2,1)}), bf16[4,1024,128]{2,1,0:T(8,128)(2,1)S(1)}, u32[]{:S(2)}, u32[]{:S(2)}) async-start(bf16[4,1024,128]{2,1,0:T(8,128)(2,1)} %bitcast.64), calls=%async_computation.3 | async-start | bytes 2097152 | tf_op jit(solution)/shard_map/all_to_all | solution.py:245
  124.1 1.2 reverse_select_fusion
  125.3 2.4 %product.5 = bf16[1024,128]{1,0:T(8,128)(2,1)S(1)} custom-call(bf16[4,1024,128]{2,1,0:T(8,128)(2,1)S(1)} %all-to-all-done.1.mine, bf16[4,1024,128]{2,1,0:T(8,128)(2,1)} %collective-permute-done.1.other, bf16[4,256,128]{2,1,0:T(8,128)(2,1)S(1)} %bitcast.61), custom_call_target="tpu_custom_call" | custom-call | flops 268435456 | bytes 4194304 | tf_op jit(solution)/shard_map/product/pallas_call | solution.py:170
  127.6 1.3 gather_fusion
  128.9 2.5 %product.4 = f32[1024,128]{1,0:T(8,128)S(1)} custom-call(bf16[4,1024,128]{2,1,0:T(8,128)(2,1)S(1)} %all-to-all-done.1.mine, bf16[4,1024,128]{2,1,0:T(8,128)(2,1)} %collective-permute-done.1.other, bf16[4,256,128]{2,1,0:T(8,128)(2,1)S(1)} %bitcast.62), custom_call_target="tpu_custom_call" | custom-call | flops 268435456 | bytes 4194304 | tf_op jit(solution)/shard_map/product/pallas_call | solution.py:170
  131.4 0.2 fusion.26
  131.7 3.2 %all-to-all-done.3 = bf16[4,1024,128]{2,1,0:T(8,128)(2,1)S(1)} async-done(((bf16[4,1024,128]{2,1,0:T(8,128)(2,1)}), bf16[4,1024,128]{2,1,0:T(8,128)(2,1)S(1)}, u32[]{:S(2)}, u32[]{:S(2)}) %all-to-all-start.3) | async-done | bytes 1048608 | tf_op jit(solution)/shard_map/all_to_all | solution.py:245
  134.9 0.9 fusion.1
  (51 shorter events, 0.5 us)
Async XLA Ops:
  6.5 25.2 %copy-start = (bf16[8,3,128,128]{3,2,1,0:T(8,128)(2,1)S(1)}, bf16[8,3,128,128]{3,2,1,0:T(8,128)(2,1)}, u32[]{:S(2)}) copy-start(bf16[8,3,128,128]{3,2,1,0:T(8,128)(2,1)} %param.18) | copy-start | bytes 2359300
  6.5 20.1 %copy-start.3 = (bf16[1024,128]{1,0:T(8,128)(2,1)S(1)}, bf16[1024,128]{1,0:T(8,128)(2,1)}, u32[]{:S(2)}) copy-start(bf16[1024,128]{1,0:T(8,128)(2,1)} %param.15) | copy-start | bytes 786436
  6.5 108.3 %all-gather.2.cloned.1.call-start = ((), (), s32[]{:S(2)}) async-start(), calls=%async_computation.4 | async-start | bytes 4456448 | tf_op jit(solution)/shard_map/all_gather | solution.py:217
  24.7 4.5 %collective-permute-start = (bf16[4,1024,128]{2,1,0:T(8,128)(2,1)S(1)}, bf16[4,1024,128]{2,1,0:T(8,128)(2,1)S(1)}, u32[]{:S(2)}, u32[]{:S(2)}) collective-permute-start(bf16[4,1024,128]{2,1,0:T(8,128)(2,1)S(1)} %all_to_all.20.mine), channel_id=1, source_target_pairs={{0,1},{1,0},{2,3},{3,2},{4,5},{5,4},{6,7},{7,6},{8,9},{9,8},{10,11... | collective-permute-start | bytes 3145736 | tf_op jit(solution)/shard_map/ppermute | solution.py:191
  26.6 4.5 %copy-start.9 = (s32[8,3]{0,1:T(4,128)S(1)}, s32[8,3]{0,1:T(4,128)}, u32[]{:S(2)}) copy-start(s32[8,3]{0,1:T(4,128)} %param.20) | copy-start | bytes 292
  26.7 4.6 %copy-start.12 = (s32[8]{0:T(128)S(1)}, s32[8]{0:T(128)}, u32[]{:S(2)}) copy-start(s32[8]{0:T(128)} %param.21) | copy-start | bytes 100
  26.7 4.7 %copy-start.10 = (s32[64]{0:T(128)S(1)}, s32[64]{0:T(128)}, u32[]{:S(2)}) copy-start(s32[64]{0:T(128)} %param.23) | copy-start | bytes 772
  26.7 4.7 %copy-start.11 = (s32[64,1]{0,1:T(1,128)S(1)}, s32[64,1]{0,1:T(1,128)}, u32[]{:S(2)}) copy-start(s32[64,1]{0,1:T(1,128)} %param.22) | copy-start | bytes 772
  32.0 25.6 %copy-start.7 = (bf16[1024,128]{1,0:T(8,128)(2,1)S(1)}, bf16[1024,128]{1,0:T(8,128)(2,1)}, u32[]{:S(2)}) copy-start(bf16[1024,128]{1,0:T(8,128)(2,1)} %param.12) | copy-start | bytes 786436
  57.6 7.3 %copy-start.13 = (s32[8]{0:T(128)S(1)}, s32[8]{0:T(128)}, u32[]{:S(2)}) copy-start(s32[8]{0:T(128)} %param.19) | copy-start | bytes 100
  57.6 9.3 %copy-start.14 = (bf16[128]{0:T(256)(128)(2,1)S(1)}, bf16[128]{0:T(256)(128)(2,1)}, u32[]{:S(2)}) copy-start(bf16[128]{0:T(256)(128)(2,1)} %param.16) | copy-start | bytes 772
  58.7 17.8 %all-to-all-start.1 = ((bf16[4,1024,128]{2,1,0:T(8,128)(2,1)}), bf16[4,1024,128]{2,1,0:T(8,128)(2,1)S(1)}, u32[]{:S(2)}, u32[]{:S(2)}) async-start(bf16[4,1024,128]{2,1,0:T(8,128)(2,1)} %broadcast_in_dim.67), calls=%async_computation.1 | async-start | bytes 2097152 | tf_op jit(solution)/shard_map/all_to_all | solution.py:187
  65.0 15.4 %collective-permute-start.2 = (bf16[4,1552,128]{2,1,0:T(8,128)(2,1)S(1)}, bf16[4,1552,128]{2,1,0:T(8,128)(2,1)}, u32[]{:S(2)}, u32[]{:S(2)}) collective-permute-start(bf16[4,1552,128]{2,1,0:T(8,128)(2,1)S(1)} %all_to_all.21.mine), channel_id=1, source_target_pairs={{0,1},{1,0},{2,3},{3,2},{4,5},{5,4},{6,7},{7,6},{8,9},{9,8},{10,11... | collective-permute-start | bytes 4767752 | tf_op jit(solution)/shard_map/ppermute | solution.py:191
  76.5 48.7 %collective-permute-start.1 = (bf16[4,1024,128]{2,1,0:T(8,128)(2,1)S(1)}, bf16[4,1024,128]{2,1,0:T(8,128)(2,1)}, u32[]{:S(2)}, u32[]{:S(2)}) collective-permute-start(bf16[4,1024,128]{2,1,0:T(8,128)(2,1)S(1)} %all-to-all-done.1.mine), channel_id=1, source_target_pairs={{0,1},{1,0},{2,3},{3,2},{4,5},{5,4},{6,7},{7,6},{8,9},{9,8},{10,11... | collective-permute-start | bytes 3145736 | tf_op jit(solution)/shard_map/ppermute | solution.py:191
  78.8 5.0 %copy-start.2 = (s32[4]{0:T(128)}, s32[4]{0:T(128)S(1)}, u32[]{:S(2)}) copy-start(s32[4]{0:T(128)S(1)} %convert_reduce_fusion.count) | copy-start | bytes 52
  83.8 1.7 %copy-start.1 = (bf16[4,24,128,128]{3,2,1,0:T(8,128)(2,1)}, bf16[4,24,128,128]{3,2,1,0:T(8,128)(2,1)S(1)}, u32[]{:S(2)}) copy-start(bf16[4,24,128,128]{3,2,1,0:T(8,128)(2,1)S(1)} %pick_tiles.1.tiles) | copy-start | bytes 9437188
  119.6 4.4 %copy-start.4 = (bf16[1024,128]{1,0:T(8,128)(2,1)S(1)}, bf16[1024,128]{1,0:T(8,128)(2,1)}, u32[]{:S(2)}) copy-start(bf16[1024,128]{1,0:T(8,128)(2,1)} %param.15) | copy-start | bytes 786436
  119.7 15.3 %all-to-all-start.3 = ((bf16[4,1024,128]{2,1,0:T(8,128)(2,1)}), bf16[4,1024,128]{2,1,0:T(8,128)(2,1)S(1)}, u32[]{:S(2)}, u32[]{:S(2)}) async-start(bf16[4,1024,128]{2,1,0:T(8,128)(2,1)} %bitcast.64), calls=%async_computation.3 | async-start | bytes 2097152 | tf_op jit(solution)/shard_map/all_to_all | solution.py:245
  128.9 2.5 %copy-start.5 = (bf16[8,128,128]{2,1,0:T(8,128)(2,1)S(1)}, bf16[8,128,128]{2,1,0:T(8,128)(2,1)}, u32[]{:S(2)}) copy-start(bf16[8,128,128]{2,1,0:T(8,128)(2,1)} %gather_fusion) | copy-start | bytes 786436
  128.9 2.5 %copy-start.8 = (bf16[8,128,128]{2,1,0:T(8,128)(2,1)S(1)}, bf16[8,128,128]{2,1,0:T(8,128)(2,1)}, u32[]{:S(2)}) copy-start(bf16[8,128,128]{2,1,0:T(8,128)(2,1)} %param.17) | copy-start | bytes 786436
  128.9 2.7 %copy-start.6 = (f32[8,128,128]{2,1,0:T(8,128)S(1)}, f32[8,128,128]{2,1,0:T(8,128)}, u32[]{:S(2)}) copy-start(f32[8,128,128]{2,1,0:T(8,128)} %get-tuple-element.21) | copy-start | bytes 1572868
Sparse Core Ops, SparseCore 0:
  31.2 83.5 all-gather.1

commit v2 on v1

v2 whole, which is shorter than its diff:
```python
import functools

import jax
import jax.numpy as jnp
from jax import lax
from jax.experimental import pallas as pl
from jax.experimental.pallas import tpu as pltpu
from jax.sharding import Mesh
from jax.sharding import PartitionSpec as P

Z, Y, X, CORE = 16, 4, 4, 2
BLK = 128
TB = 8
HT = 3
REFS = TB * HT
HALF = REFS // CORE
META = 16
GROUP = 4


def pick_kernel(notes, place, mine, other, table, picked, buf, sem, out_sem):
    me, core = place[0], place[1]
    counts = []
    for peer in range(Y):

        def step(ref, count):
            owner, block = notes[peer, ref], notes[peer, REFS + ref]
            here = jnp.logical_and(owner >= 0, lax.rem(owner, Y) == me)
            at = pl.ds(pl.multiple_of(lax.rem(ref, HALF) * BLK, BLK), BLK)
            from_mine = lax.div(ref, HALF) == core

            @pl.when(here)
            def _():
                table[peer, count] = lax.div(owner, Y) * TB + block
                table[peer, REFS + count] = peer * TB + lax.div(ref, HT)

            @pl.when(jnp.logical_and(here, from_mine))
            def _():
                pltpu.make_async_copy(mine.at[peer, at], buf.at[peer, count], sem.at[peer, count]).start()

            @pl.when(jnp.logical_and(here, jnp.logical_not(from_mine)))
            def _():
                pltpu.make_async_copy(other.at[peer, at], buf.at[peer, count], sem.at[peer, count]).start()

            return count + here.astype(jnp.int32)

        count = lax.fori_loop(0, REFS, step, jnp.int32(0))
        counts.append(count)
        table[peer, 2 * REFS] = count
        table[peer, 2 * REFS + 1] = me

        @pl.loop(count, REFS)
        def _(i):
            table[peer, i] = 0
            table[peer, REFS + i] = Y * TB

    def out_copy(peer, group):
        at = pl.ds(group * GROUP, GROUP)
        return pltpu.make_async_copy(buf.at[peer, at], picked.at[peer, at], out_sem.at[peer, group])

    for peer in range(Y):

        @pl.loop(0, (counts[peer] + GROUP - 1) // GROUP)
        def _(group):
            for u in range(GROUP):
                i = group * GROUP + u

                @pl.when(i < counts[peer])
                def _():
                    pltpu.make_async_copy(mine.at[peer, pl.ds(0, BLK)], buf.at[peer, i], sem.at[peer, i]).wait()

            out_copy(peer, group).start()

    for peer in range(Y):

        @pl.loop(0, (counts[peer] + GROUP - 1) // GROUP)
        def _(group):
            out_copy(peer, group).wait()


def partial_kernel(
    table, blocks, tiles, sent, own, block_buf, tile_buf, sent_buf, total, block_sem, tile_sem, out_sem
):
    count = [table[peer, 2 * REFS] for peer in range(Y)]
    me = table[0, 2 * REFS + 1]

    def groups(peer):
        return (count[peer] + GROUP - 1) // GROUP

    def block_copy(peer, i):
        row = pl.multiple_of(table[peer, i] * BLK, BLK)
        return pltpu.make_async_copy(blocks.at[pl.ds(row, BLK)], block_buf.at[peer, i], block_sem.at[peer, i])

    def tile_copy(peer, group):
        at = pl.ds(group * GROUP, GROUP)
        return pltpu.make_async_copy(tiles.at[peer, at], tile_buf.at[peer, at], tile_sem.at[peer, group])

    for peer in range(Y):

        @pl.loop(0, groups(peer))
        def _(group):
            tile_copy(peer, group).start()
            for u in range(GROUP):
                i = group * GROUP + u

                @pl.when(i < count[peer])
                def _():
                    block_copy(peer, i).start()

    total[...] = jnp.zeros_like(total)
    copies = []
    for peer in range(Y):

        @pl.loop(0, groups(peer))
        def _(group):
            members = [group * GROUP + u for u in range(GROUP)]
            tile_copy(peer, group).wait()
            for i in members:

                @pl.when(i < count[peer])
                def _():
                    block_copy(peer, i).wait()

            products = [
                jnp.dot(tile_buf[peer, i], block_buf[peer, i], preferred_element_type=jnp.float32) for i in members
            ]
            for i, part in zip(members, products):
                total[table[peer, REFS + i]] += part

        at = pl.ds(peer * TB, TB)
        sent_buf[at] = jnp.where(me == peer, 0.0, total[at]).astype(sent.dtype)
        copies.append(pltpu.make_async_copy(sent_buf.at[at], sent.at[at], out_sem.at[peer]))
        copies[-1].start()
    copies.append(pltpu.make_async_copy(total.at[pl.ds(me * TB, TB)], own, out_sem.at[Y]))
    copies[-1].start()
    for copy in copies:
        copy.wait()


def partial_sums(notes, place, blocks, mine, other):
    smem, hbm = pl.BlockSpec(memory_space=pltpu.SMEM), pl.BlockSpec(memory_space=pltpu.HBM)
    table, picked = pl.pallas_call(
        pick_kernel,
        out_shape=(
            jax.ShapeDtypeStruct((Y, 2 * REFS + 2), jnp.int32),
            jax.ShapeDtypeStruct((Y, REFS, BLK, BLK), jnp.bfloat16),
        ),
        in_specs=[smem] * 2 + [hbm] * 2,
        out_specs=(smem, hbm),
        scratch_shapes=[
            pltpu.VMEM((Y, REFS, BLK, BLK), jnp.bfloat16),
            pltpu.SemaphoreType.DMA((Y, REFS)),
            pltpu.SemaphoreType.DMA((Y, REFS // GROUP)),
        ],
        compiler_params=pltpu.CompilerParams(vmem_limit_bytes=8 * 1024 * 1024),
        cost_estimate=pl.CostEstimate(flops=0, bytes_accessed=4 * 2**20, transcendentals=0),
        name="pick_tiles",
    )(notes, place, mine, other)
    return pl.pallas_call(
        partial_kernel,
        out_shape=(
            jax.ShapeDtypeStruct((Y * TB, BLK, BLK), jnp.bfloat16),
            jax.ShapeDtypeStruct((TB, BLK, BLK), jnp.float32),
        ),
        in_specs=[smem] + [hbm] * 2,
        out_specs=(hbm, hbm),
        scratch_shapes=[
            pltpu.VMEM((Y, REFS, BLK, BLK), jnp.bfloat16),
            pltpu.VMEM((Y, REFS, BLK, BLK), jnp.bfloat16),
            pltpu.VMEM((Y * TB, BLK, BLK), jnp.bfloat16),
            pltpu.VMEM((Y * TB + 1, BLK, BLK), jnp.float32),
            pltpu.SemaphoreType.DMA((Y, REFS)),
            pltpu.SemaphoreType.DMA((Y, REFS // GROUP)),
            pltpu.SemaphoreType.DMA((Y + 1,)),
        ],
        compiler_params=pltpu.CompilerParams(vmem_limit_bytes=60 * 1024 * 1024),
        cost_estimate=pl.CostEstimate(flops=REFS * 2 * BLK**3, bytes_accessed=4 * 2**20, transcendentals=0),
        name="partial_sums",
    )(table, blocks, picked)


def product_kernel(last, parts, weight, base, out):
    rows = 256

    @pl.loop(0, out.shape[0] // rows)
    def _(step):
        at = pl.ds(pl.multiple_of(step * rows, rows), rows)
        total = base[at]
        for i in range(X // 2):
            pair = jnp.concatenate([parts[2 * i, at], parts[2 * i + 1, at]], axis=1)
            total = total + jnp.dot(pair, weight[i], preferred_element_type=jnp.float32)
        out[at] = jnp.maximum(total, 0.0).astype(out.dtype) if last else total


def add_product(base, parts, weight, last=False):
    vmem = pl.BlockSpec(memory_space=pltpu.VMEM)
    return pl.pallas_call(
        functools.partial(product_kernel, last),
        out_shape=jax.ShapeDtypeStruct(base.shape, jnp.bfloat16 if last else jnp.float32),
        in_specs=[vmem] * 3,
        out_specs=vmem,
        compiler_params=pltpu.CompilerParams(vmem_limit_bytes=16 * 1024 * 1024),
        cost_estimate=pl.CostEstimate(flops=base.size * 1024, bytes_accessed=2 * 2**20, transcendentals=0),
        name="add_product",
    )(parts, weight, base)


def rows_of_core(weight, core):
    parts = weight.reshape(X, CORE, BLK, weight.shape[1])
    return jnp.where(core == 0, parts[:, 0], parts[:, 1]).reshape(X // 2, 2 * BLK, weight.shape[1])


def to_all(array, axis, size):
    return lax.all_to_all(jnp.broadcast_to(array[None], (size,) + array.shape), axis, 0, 0, tiled=True)


def swap_cores(array):
    return lax.ppermute(array, "core", [(0, 1), (1, 0)])


def all_columns(array):
    mine = to_all(array, "x", X)
    return mine, swap_cores(mine)


def body(
    features,
    history,
    w_root,
    w_neigh,
    bias,
    local_tiles,
    halo_tiles,
    local_src,
    halo_src,
    halo_count,
    halo_peer,
    halo_block,
):
    rows, columns = features.shape
    my_z, my_y, my_core = lax.axis_index("z"), lax.axis_index("y"), lax.axis_index("core")

    column_blocks = lax.all_gather(history, "z", axis=0, tiled=True)

    owners = (my_z * Y + my_y + 1 + halo_peer[:, 0]) % (Z * Y)
    hits = halo_src.reshape(REFS, 1) == jnp.arange(halo_block.shape[0], dtype=jnp.int32)[None, :]
    used = (lax.broadcasted_iota(jnp.int32, (TB, HT), 1) < halo_count[:, None]).reshape(REFS)
    code = jnp.sum(jnp.where(hits, (owners * TB + halo_block)[None, :], 0), axis=1)
    code = jnp.where(used, code, -TB)
    notes = jnp.stack([code // TB, code % TB])
    notes = jnp.pad(notes, ((0, META - 2), (0, BLK - REFS))).astype(jnp.bfloat16)
    share = lax.dynamic_slice_in_dim(halo_tiles.reshape(REFS * BLK, BLK), my_core * HALF * BLK, HALF * BLK)
    mine = to_all(jnp.concatenate([share, notes]), "y", Y)
    other = swap_cores(mine)
    told = mine[:, HALF * BLK : HALF * BLK + 2, :REFS].astype(jnp.int32).reshape(Y, 2 * REFS)
    place = jnp.stack([my_y, my_core])

    own_blocks = features.reshape(TB, BLK, columns)[local_src]
    local_part = jnp.einsum("bij,bjc->bic", local_tiles, own_blocks, preferred_element_type=jnp.float32)
    base = jnp.broadcast_to(bias.astype(jnp.float32)[None], (rows, columns))
    mine_f, other_f = all_columns(features)
    base = add_product(base, mine_f, rows_of_core(w_root, my_core))
    base = add_product(base, other_f, rows_of_core(w_root, 1 - my_core))
    neigh, neigh_other = rows_of_core(w_neigh, my_core), rows_of_core(w_neigh, 1 - my_core)
    column_blocks, base, local_part, neigh, neigh_other = lax.optimization_barrier(
        (column_blocks, base, local_part, neigh, neigh_other)
    )

    sent, own = partial_sums(told, place, column_blocks, mine, other)
    came = lax.all_to_all(sent.reshape(Y, rows, columns), "y", 0, 0, tiled=True)
    total = lax.optimization_barrier(local_part + own).reshape(rows, columns)
    for i in range(Y):
        total = total + came[i].astype(jnp.float32)
    mine_a = to_all(total.astype(jnp.bfloat16), "x", X)
    other_a = swap_cores(mine_a)
    base = add_product(base, mine_a, neigh)
    return add_product(base, other_a, neigh_other, last=True)


def solution(mesh):
    chips = Mesh(mesh.devices.reshape(Z, Y, X, CORE), ("z", "y", "x", "core"))
    dom, feat = ("z", "y"), ("x", "core")
    in_specs = (
        P(dom, feat),
        P(dom, feat),
        P(None, feat),
        P(None, feat),
        P(feat),
        P(dom, None, None),
        P(dom, None, None, None),
        P(dom),
        P(dom, None),
        P(dom),
        P(dom, None),
        P(dom),
    )
    return jax.shard_map(body, mesh=chips, in_specs=in_specs, out_specs=P(dom, feat), check_vma=False)
```

time: 143 us -> 143 us (level)
  the two profiles are of different devices: /device:TPU:4 before, /device:TPU:1 now
where the time goes in v2:
time: 143 us; the launch traced here: 142 us
  starting transfers between devices  35.1 us (25%)
  blocking collectives  34.9 us (24%)
  waiting for transfers between devices  21.9 us (15%)
  Pallas kernels  16.9 us (12%)
  between operations  13.6 us (10%)
  local copies, waits for them, and re-layouts  11.7 us (8%)
  other arithmetic  6.02 us (4%)
  matrix products  2.1 us (1%)
    all_to_all x2, blocking collectives, to_all(): lax.all_to_all(jnp.broadcast_to(array[None], (size,) + array.shape), axis...  34.9 us
    ppermute x3, starting transfers between devices, swap_cores(): return lax.ppermute(array, 'core', [(0, 1), (1, 0)])  22.9 us
    all_to_all x1, waiting for transfers between devices, to_all(): lax.all_to_all(jnp.broadcast_to(array[None], (size,) + array.shape), axis...  8.83 us
    all_to_all x1, waiting for transfers between devices, body(): came = lax.all_to_all(sent.reshape(Y, rows, columns), 'y', 0, 0, tiled=True)  8.64 us
    all_to_all x1, starting transfers between devices, to_all(): lax.all_to_all(jnp.broadcast_to(array[None], (size,) + array.shape), axis...  7.5 us
    pallas_call x1, Pallas kernels, partial_sums(): pl.pallas_call(pick_kernel, out_shape=(jax.ShapeDtypeStruct((Y, 2 * REFS...  6.75 us
    unnamed x25, local copies, waits for them, and re-layouts  5.77 us
    pallas_call x4, Pallas kernels, add_product(): pl.pallas_call(functools.partial(product_kernel, last), out_shape=jax.Sha...  5.39 us
  transfers between devices with their start and end apart: 6, of which 4 were waited for; matrix products, arithmetic and copies ran while one was open for 10% of the time, Pallas kernels for 7%

profile of v2, /device:TPU:1, one launch (start us, length us, event | category | flops | bytes accessed | tf_op | source)
XLA Modules:
  0.0 142.2 jit_solution(17071481249009455272)
XLA Ops:
  6.5 0.7 all-gather.2.cloned.1.call-update
  7.3 0.8 copy.32
  8.1 0.7 iota_compare_fusion.3
  8.9 0.7 fusion.12
  10.2 21.4 %all_to_all.20.mine = bf16[4,1552,128]{2,1,0:T(8,128)(2,1)S(1)} all-to-all(bf16[4,1552,128]{2,1,0:T(8,128)(2,1)S(1)} %broadcast_in_dim.54), channel_id=1, replica_groups=mesh['z'=16,'y'=4,'x'=4,'core'=2] {'y'}, dimensions={0} | all-to-all | bytes 3178496 | tf_op jit(solution)/shard_map/all_to_all | solution.py:214
  31.5 1.1 broadcast_in_dim.28
  32.7 7.5 %all-to-all-start = ((bf16[4,1024,128]{2,1,0:T(8,128)(2,1)}), bf16[4,1024,128]{2,1,0:T(8,128)(2,1)S(1)}, u32[]{:S(2)}, u32[]{:S(2)}) async-start(bf16[4,1024,128]{2,1,0:T(8,128)(2,1)} %broadcast_in_dim.28), calls=%async_computation | async-start | bytes 2097152 | tf_op jit(solution)/shard_map/all_to_all | solution.py:214
  40.2 4.1 %collective-permute-start.1 = (bf16[4,1552,128]{2,1,0:T(8,128)(2,1)S(1)}, bf16[4,1552,128]{2,1,0:T(8,128)(2,1)}, u32[]{:S(2)}, u32[]{:S(2)}) collective-permute-start(bf16[4,1552,128]{2,1,0:T(8,128)(2,1)S(1)} %all_to_all.20.mine), channel_id=1, source_target_pairs={{0,1},{1,0},{2,3},{3,2},{4,5},{5,4},{6,7},{7,6},{8,9},{9,8},{10,11... | collective-permute-start | bytes 4767752 | tf_op jit(solution)/shard_map/ppermute | solution.py:218
  44.3 8.8 %all-to-all-done.parts = bf16[4,1024,128]{2,1,0:T(8,128)(2,1)S(1)} async-done(((bf16[4,1024,128]{2,1,0:T(8,128)(2,1)}), bf16[4,1024,128]{2,1,0:T(8,128)(2,1)S(1)}, u32[]{:S(2)}, u32[]{:S(2)}) %all-to-all-start) | async-done | bytes 1048608 | tf_op jit(solution)/shard_map/all_to_all | solution.py:214
  53.1 5.0 %collective-permute-start = (bf16[4,1024,128]{2,1,0:T(8,128)(2,1)S(1)}, bf16[4,1024,128]{2,1,0:T(8,128)(2,1)}, u32[]{:S(2)}, u32[]{:S(2)}) collective-permute-start(bf16[4,1024,128]{2,1,0:T(8,128)(2,1)S(1)} %all-to-all-done.parts), channel_id=1, source_target_pairs={{0,1},{1,0},{2,3},{3,2},{4,5},{5,4},{6,7},{7,6},{8,9},{9,8},{10,11... | collective-permute-start | bytes 3145736 | tf_op jit(solution)/shard_map/ppermute | solution.py:218
  58.2 2.2 %gather_fusion = bf16[8,128,128]{2,1,0:T(8,128)(2,1)} fusion(bf16[8,128,128]{2,1,0:T(8,128)(2,1)} %bitcast.69, s32[1024]{0:T(1024)S(1)} %pad_clamp_fusion), kind=kCustom, calls=%fused_computation | custom fusion | bytes 524320 | tf_op jit(solution)/shard_map/gather | solution.py:258
  61.1 1.8 %broadcast_select_fusion.1 = (bf16[4,1,128,128]{3,2,0,1:T(8,128)(2,1)S(1)}, bf16[4,1,128,128]{3,2,0,1:T(8,128)(2,1)}, bf16[4,1,128,128]{3,2,0,1:T(8,128)(2,1)S(1)}, bf16[4,1,128,128]{3,2,0,1:T(8,128)(2,1)}) fusion(pred[]{:T(512)S(6)} %eq.28, bf16[4,2,128,128]{3,2,1,0:T(8,128)(2,1)} %bitcast.71, pred[]{:T(512)S(6)} %eq.27, bf16[4,2,128,128]{3,2,1,0:T(8,128)(2,1)} %bitcast.72), kind=kLoop, calls=%fused_computation.14 | loop fusion | flops 262144 | bytes 1048578 | tf_op jit(solution)/shard_map/jit(_where)/select_n | solution.py:210
  62.9 2.1 %convolution_bitcast_fusion = f32[8,128,128]{2,1,0:T(8,128)} fusion(bf16[8,128,128]{2,1,0:T(8,128)(2,1)} %param.17, bf16[8,128,128]{2,1,0:T(8,128)(2,1)} %gather_fusion), kind=kOutput, calls=%fused_computation.1 | convolution fusion | flops 33554432 | bytes 1048576 | tf_op jit(solution)/shard_map/bij,bjc->bic/dot_general | solution.py:259
  65.0 0.7 broadcast_in_dim.29.base
  65.7 0.9 add_product.4.base
  66.6 0.8 copy-done.2
  67.9 1.4 reshape.168.notes
  69.3 1.0 copy-done.3
  70.4 0.9 copy-done.4
  71.3 2.1 %add_product.5.base = f32[1024,128]{1,0:T(8,128)S(1)} custom-call(bf16[4,1024,128]{2,1,0:T(8,128)(2,1)} %collective-permute-done.parts, bf16[2,256,128]{2,1,0:T(8,128)(2,1)S(1)} %bitcast.65, f32[1024,128]{1,0:T(8,128)S(1)} %copy-done.3), custom_call_target="tpu_custom_call" | custom-call | flops 134217728 | bytes 2097152 | tf_op jit(solution)/shard_map/add_product/pallas_call | solution.py:197
  73.4 6.7 %pick_tiles.1 = (s32[4,50]{1,0:T(4,128)S(1)}, bf16[4,24,128,128]{3,2,1,0:T(8,128)(2,1)S(1)}) custom-call(s32[4,48]{1,0:T(4,128)S(1)} %copy-done.6, s32[2]{0:T(128)S(1)} %copy-done.8, bf16[4,1552,128]{2,1,0:T(8,128)(2,1)S(1)} %all_to_all.20.mine, bf16[4,1552,128]{2,1,0:T(8,128)(2,1)} %collective-permute-done.1.other), custom_call_target="tpu_custom_call" | custom-call | bytes 4194304 | tf_op jit(solution)/shard_map/pick_tiles/pallas_call | solution.py:142
  80.2 1.7 %copy-done.1 = bf16[4,24,128,128]{3,2,1,0:T(8,128)(2,1)} copy-done((bf16[4,24,128,128]{3,2,1,0:T(8,128)(2,1)}, bf16[4,24,128,128]{3,2,1,0:T(8,128)(2,1)S(1)}, u32[]{:S(2)}) %copy-start.1) | copy-done | bytes 3145752
  82.4 2.3 %all-gather.2.cloned.1.call-done.blocks = bf16[16384,128]{1,0:T(8,128)(2,1)} async-done(((bf16[1024,128]{1,0:T(8,128)(2,1)}), bf16[16384,128]{1,0:T(8,128)(2,1)}) %all-gather.2.cloned.1.call-update) | async-done | bytes 4194320 | tf_op jit(solution)/shard_map/all_gather | solution.py:243
  84.7 4.7 %partial_sums.1 = (bf16[32,128,128]{2,1,0:T(8,128)(2,1)}, f32[8,128,128]{2,1,0:T(8,128)}) custom-call(s32[4,50]{1,0:T(4,128)} %copy-done.7, bf16[16384,128]{1,0:T(8,128)(2,1)} %all-gather.2.cloned.1.call-done.blocks, bf16[4,24,128,128]{3,2,1,0:T(8,128)(2,1)} %copy-done.1), custom_call_target="tpu_custom_call" | custom-call | flops 100663296 | bytes 4194304 | tf_op jit(solution)/shard_map/partial_sums/pallas_call | solution.py:159
  89.4 4.7 %all-to-all-start.2 = ((bf16[4,1024,128]{2,1,0:T(8,128)(2,1)}), bf16[4,1024,128]{2,1,0:T(8,128)(2,1)S(1)}, u32[]{:S(2)}, u32[]{:S(2)}) async-start(bf16[4,1024,128]{2,1,0:T(8,128)(2,1)} %bitcast.70), calls=%async_computation.2 | async-start | bytes 2097152 | tf_op jit(solution)/shard_map/all_to_all | solution.py:270
  94.1 1.1 add.82
  95.2 8.6 %all-to-all-done.2 = bf16[4,1024,128]{2,1,0:T(8,128)(2,1)S(1)} async-done(((bf16[4,1024,128]{2,1,0:T(8,128)(2,1)}), bf16[4,1024,128]{2,1,0:T(8,128)(2,1)S(1)}, u32[]{:S(2)}, u32[]{:S(2)}) %all-to-all-start.2) | async-done | bytes 1048608 | tf_op jit(solution)/shard_map/all_to_all | solution.py:270
  104.2 13.5 %all_to_all.21.parts = bf16[4,1024,128]{2,1,0:T(8,128)(2,1)S(1)} all-to-all(bf16[4,1024,128]{2,1,0:T(8,128)(2,1)S(1)} %broadcast_in_dim.56), channel_id=1, replica_groups=mesh['z'=16,'y'=4,'x'=4,'core'=2] {'x'}, dimensions={0} | all-to-all | bytes 2097152 | tf_op jit(solution)/shard_map/all_to_all | solution.py:214
  117.7 13.8 %collective-permute-start.2 = (bf16[4,1024,128]{2,1,0:T(8,128)(2,1)S(1)}, bf16[4,1024,128]{2,1,0:T(8,128)(2,1)S(1)}, u32[]{:S(2)}, u32[]{:S(2)}) collective-permute-start(bf16[4,1024,128]{2,1,0:T(8,128)(2,1)S(1)} %all_to_all.21.parts), channel_id=1, source_target_pairs={{0,1},{1,0},{2,3},{3,2},{4,5},{5,4},{6,7},{7,6},{8,9},{9,8},{10,11... | collective-permute-start | bytes 3145736 | tf_op jit(solution)/shard_map/ppermute | solution.py:218
  131.5 0.8 add_product.6.base
  132.3 1.4 collective-permute-done.2.parts
  133.8 1.6 %add_product.7 = bf16[1024,128]{1,0:T(8,128)(2,1)} custom-call(bf16[4,1024,128]{2,1,0:T(8,128)(2,1)S(1)} %collective-permute-done.2.parts, bf16[2,256,128]{2,1,0:T(8,128)(2,1)S(1)} %bitcast.67, f32[1024,128]{1,0:T(8,128)S(1)} %add_product.6.base), custom_call_target="tpu_custom_call" | custom-call | flops 134217728 | bytes 2097152 | tf_op jit(solution)/shard_map/add_product/pallas_call | solution.py:197
  (38 shorter events, 2.8 us)
Async XLA Ops:
  6.5 3.3 %copy-start = (bf16[8,3,128,128]{3,2,1,0:T(8,128)(2,1)S(1)}, bf16[8,3,128,128]{3,2,1,0:T(8,128)(2,1)}, u32[]{:S(2)}) copy-start(bf16[8,3,128,128]{3,2,1,0:T(8,128)(2,1)} %param.18) | copy-start | bytes 2359300
  6.5 78.1 %all-gather.2.cloned.1.call-start = ((), (), s32[]{:S(2)}) async-start(), calls=%async_computation.4 | async-start | bytes 4456448 | tf_op jit(solution)/shard_map/all_gather | solution.py:243
  10.1 21.4 %copy-start.10 = (bf16[1024,128]{1,0:T(8,128)(2,1)S(1)}, bf16[1024,128]{1,0:T(8,128)(2,1)}, u32[]{:S(2)}) copy-start(bf16[1024,128]{1,0:T(8,128)(2,1)} %param.12) | copy-start | bytes 786436
  31.5 26.6 %copy-start.11 = (s32[8]{0:T(128)S(1)}, s32[8]{0:T(128)}, u32[]{:S(2)}) copy-start(s32[8]{0:T(128)} %param.19) | copy-start | bytes 100
  32.7 20.4 %all-to-all-start = ((bf16[4,1024,128]{2,1,0:T(8,128)(2,1)}), bf16[4,1024,128]{2,1,0:T(8,128)(2,1)S(1)}, u32[]{:S(2)}, u32[]{:S(2)}) async-start(bf16[4,1024,128]{2,1,0:T(8,128)(2,1)} %broadcast_in_dim.28), calls=%async_computation | async-start | bytes 2097152 | tf_op jit(solution)/shard_map/all_to_all | solution.py:214
  40.2 33.2 %collective-permute-start.1 = (bf16[4,1552,128]{2,1,0:T(8,128)(2,1)S(1)}, bf16[4,1552,128]{2,1,0:T(8,128)(2,1)}, u32[]{:S(2)}, u32[]{:S(2)}) collective-permute-start(bf16[4,1552,128]{2,1,0:T(8,128)(2,1)S(1)} %all_to_all.20.mine), channel_id=1, source_target_pairs={{0,1},{1,0},{2,3},{3,2},{4,5},{5,4},{6,7},{7,6},{8,9},{9,8},{10,11... | collective-permute-start | bytes 4767752 | tf_op jit(solution)/shard_map/ppermute | solution.py:218
  53.1 16.2 %collective-permute-start = (bf16[4,1024,128]{2,1,0:T(8,128)(2,1)S(1)}, bf16[4,1024,128]{2,1,0:T(8,128)(2,1)}, u32[]{:S(2)}, u32[]{:S(2)}) collective-permute-start(bf16[4,1024,128]{2,1,0:T(8,128)(2,1)S(1)} %all-to-all-done.parts), channel_id=1, source_target_pairs={{0,1},{1,0},{2,3},{3,2},{4,5},{5,4},{6,7},{7,6},{8,9},{9,8},{10,11... | collective-permute-start | bytes 3145736 | tf_op jit(solution)/shard_map/ppermute | solution.py:218
  66.6 0.8 copy-start.2
  69.3 4.1 %copy-start.6 = (s32[4,48]{1,0:T(4,128)S(1)}, s32[4,48]{1,0:T(4,128)}, u32[]{:S(2)}) copy-start(s32[4,48]{1,0:T(4,128)} %reshape.168.notes) | copy-start | bytes 2308
  69.3 4.1 %copy-start.8 = (s32[2]{0:T(128)S(1)}, s32[2]{0:T(128)}, u32[]{:S(2)}) copy-start(s32[2]{0:T(128)} %pad_add_fusion.place) | copy-start | bytes 28
  69.3 1.0 copy-start.3
  70.4 0.9 copy-start.4
  80.2 1.7 %copy-start.1 = (bf16[4,24,128,128]{3,2,1,0:T(8,128)(2,1)}, bf16[4,24,128,128]{3,2,1,0:T(8,128)(2,1)S(1)}, u32[]{:S(2)}) copy-start(bf16[4,24,128,128]{3,2,1,0:T(8,128)(2,1)S(1)} %get-tuple-element.17.tiles) | copy-start | bytes 9437188
  81.9 0.6 copy-start.7
  89.4 4.7 %copy-start.9 = (f32[8,128,128]{2,1,0:T(8,128)S(1)}, f32[8,128,128]{2,1,0:T(8,128)}, u32[]{:S(2)}) copy-start(f32[8,128,128]{2,1,0:T(8,128)} %convolution_bitcast_fusion) | copy-start | bytes 1572868
  89.4 14.4 %all-to-all-start.2 = ((bf16[4,1024,128]{2,1,0:T(8,128)(2,1)}), bf16[4,1024,128]{2,1,0:T(8,128)(2,1)S(1)}, u32[]{:S(2)}, u32[]{:S(2)}) async-start(bf16[4,1024,128]{2,1,0:T(8,128)(2,1)} %bitcast.70), calls=%async_computation.2 | async-start | bytes 2097152 | tf_op jit(solution)/shard_map/all_to_all | solution.py:270
  117.7 16.1 %copy-start.5 = (bf16[4,1,128,128]{3,2,0,1:T(8,128)(2,1)S(1)}, bf16[4,1,128,128]{3,2,0,1:T(8,128)(2,1)}, u32[]{:S(2)}) copy-start(bf16[4,1,128,128]{3,2,0,1:T(8,128)(2,1)} %get-tuple-element.30) | copy-start | bytes 393220
  117.7 16.1 %collective-permute-start.2 = (bf16[4,1024,128]{2,1,0:T(8,128)(2,1)S(1)}, bf16[4,1024,128]{2,1,0:T(8,128)(2,1)S(1)}, u32[]{:S(2)}, u32[]{:S(2)}) collective-permute-start(bf16[4,1024,128]{2,1,0:T(8,128)(2,1)S(1)} %all_to_all.21.parts), channel_id=1, source_target_pairs={{0,1},{1,0},{2,3},{3,2},{4,5},{5,4},{6,7},{7,6},{8,9},{9,8},{10,11... | collective-permute-start | bytes 3145736 | tf_op jit(solution)/shard_map/ppermute | solution.py:218
Sparse Core Ops, SparseCore 0:
  9.4 75.2 all-gather.1

commit v3 on v2

--- a/solution.py
+++ b/solution.py
@@ -79,7 +79,7 @@
 
 
 def partial_kernel(
-    table, blocks, tiles, sent, own, block_buf, tile_buf, sent_buf, total, block_sem, tile_sem, out_sem
+    table, blocks, tiles, local, sent, block_buf, tile_buf, local_buf, sent_buf, total, block_sem, tile_sem, out_sem
 ):
     count = [table[peer, 2 * REFS] for peer in range(Y)]
     me = table[0, 2 * REFS + 1]
@@ -107,6 +107,8 @@
                 def _():
                     block_copy(peer, i).start()
 
+    local_copy = pltpu.make_async_copy(local, local_buf, out_sem.at[Y])
+    local_copy.start()
     total[...] = jnp.zeros_like(total)
     copies = []
     for peer in range(Y):
@@ -127,17 +129,20 @@
             for i, part in zip(members, products):
                 total[table[peer, REFS + i]] += part
 
+        @pl.when(me == peer)
+        def _():
+            local_copy.wait()
+            total[pl.ds(peer * TB, TB)] += local_buf[...]
+
         at = pl.ds(peer * TB, TB)
-        sent_buf[at] = jnp.where(me == peer, 0.0, total[at]).astype(sent.dtype)
+        sent_buf[at] = total[at].astype(sent.dtype)
         copies.append(pltpu.make_async_copy(sent_buf.at[at], sent.at[at], out_sem.at[peer]))
         copies[-1].start()
-    copies.append(pltpu.make_async_copy(total.at[pl.ds(me * TB, TB)], own, out_sem.at[Y]))
-    copies[-1].start()
     for copy in copies:
         copy.wait()
 
 
-def partial_sums(notes, place, blocks, mine, other):
+def partial_sums(notes, place, blocks, local, mine, other):
     smem, hbm = pl.BlockSpec(memory_space=pltpu.SMEM), pl.BlockSpec(memory_space=pltpu.HBM)
     table, picked = pl.pallas_call(
         pick_kernel,
@@ -158,15 +163,13 @@
     )(notes, place, mine, other)
     return pl.pallas_call(
         partial_kernel,
-        out_shape=(
-            jax.ShapeDtypeStruct((Y * TB, BLK, BLK), jnp.bfloat16),
-            jax.ShapeDtypeStruct((TB, BLK, BLK), jnp.float32),
-        ),
-        in_specs=[smem] + [hbm] * 2,
-        out_specs=(hbm, hbm),
+        out_shape=jax.ShapeDtypeStruct((Y * TB, BLK, BLK), jnp.bfloat16),
+        in_specs=[smem] + [hbm] * 3,
+        out_specs=hbm,
         scratch_shapes=[
             pltpu.VMEM((Y, REFS, BLK, BLK), jnp.bfloat16),
             pltpu.VMEM((Y, REFS, BLK, BLK), jnp.bfloat16),
+            pltpu.VMEM((TB, BLK, BLK), jnp.float32),
             pltpu.VMEM((Y * TB, BLK, BLK), jnp.bfloat16),
             pltpu.VMEM((Y * TB + 1, BLK, BLK), jnp.float32),
             pltpu.SemaphoreType.DMA((Y, REFS)),
@@ -176,20 +179,16 @@
         compiler_params=pltpu.CompilerParams(vmem_limit_bytes=60 * 1024 * 1024),
         cost_estimate=pl.CostEstimate(flops=REFS * 2 * BLK**3, bytes_accessed=4 * 2**20, transcendentals=0),
         name="partial_sums",
-    )(table, blocks, picked)
+    )(table, blocks, picked, local)
 
 
 def product_kernel(last, parts, weight, base, out):
-    rows = 256
-
-    @pl.loop(0, out.shape[0] // rows)
-    def _(step):
-        at = pl.ds(pl.multiple_of(step * rows, rows), rows)
-        total = base[at]
-        for i in range(X // 2):
-            pair = jnp.concatenate([parts[2 * i, at], parts[2 * i + 1, at]], axis=1)
-            total = total + jnp.dot(pair, weight[i], preferred_element_type=jnp.float32)
-        out[at] = jnp.maximum(total, 0.0).astype(out.dtype) if last else total
+    pairs = [jnp.concatenate([parts[2 * i], parts[2 * i + 1]], axis=1) for i in range(X // 2)]
+    for x in range(X):
+        total = base[x]
+        for i, pair in enumerate(pairs):
+            total = total + jnp.dot(pair, weight[x, i], preferred_element_type=jnp.float32)
+        out[x] = jnp.maximum(total, 0.0).astype(out.dtype) if last else total
 
 
 def add_product(base, parts, weight, last=False):
@@ -205,9 +204,9 @@
     )(parts, weight, base)
 
 
-def rows_of_core(weight, core):
-    parts = weight.reshape(X, CORE, BLK, weight.shape[1])
-    return jnp.where(core == 0, parts[:, 0], parts[:, 1]).reshape(X // 2, 2 * BLK, weight.shape[1])
+def rows_of_core(weights, core):
+    parts = weights.reshape(X, X, CORE, BLK, BLK)
+    return jnp.where(core == 0, parts[:, :, 0], parts[:, :, 1]).reshape(X, X // 2, 2 * BLK, BLK)
 
 
 def to_all(array, axis, size):
@@ -218,9 +217,9 @@
     return lax.ppermute(array, "core", [(0, 1), (1, 0)])
 
 
-def all_columns(array):
-    mine = to_all(array, "x", X)
-    return mine, swap_cores(mine)
+def of_ring(array, x):
+    came = [array] + [lax.ppermute(array, "x", [(i, (i + r) % X) for i in range(X)]) for r in range(1, X)]
+    return jnp.stack(came)[(x - jnp.arange(X)) % X]
 
 
 def body(
@@ -242,6 +241,11 @@
 
     column_blocks = lax.all_gather(history, "z", axis=0, tiled=True)
 
+    depth = w_root.shape[0]
+    bias_rows = jnp.pad(bias[None], ((0, META - 1), (0, 0)))
+    weights = of_ring(jnp.concatenate([w_root, w_neigh, bias_rows]), lax.axis_index("x"))
+    root, neigh, bias_row = weights[:, :depth], weights[:, depth : 2 * depth], weights[:, 2 * depth : 2 * depth + 1]
+
     owners = (my_z * Y + my_y + 1 + halo_peer[:, 0]) % (Z * Y)
     hits = halo_src.reshape(REFS, 1) == jnp.arange(halo_block.shape[0], dtype=jnp.int32)[None, :]
     used = (lax.broadcasted_iota(jnp.int32, (TB, HT), 1) < halo_count[:, None]).reshape(REFS)
@@ -257,24 +261,24 @@
 
     own_blocks = features.reshape(TB, BLK, columns)[local_src]
     local_part = jnp.einsum("bij,bjc->bic", local_tiles, own_blocks, preferred_element_type=jnp.float32)
-    base = jnp.broadcast_to(bias.astype(jnp.float32)[None], (rows, columns))
-    mine_f, other_f = all_columns(features)
-    base = add_product(base, mine_f, rows_of_core(w_root, my_core))
-    base = add_product(base, other_f, rows_of_core(w_root, 1 - my_core))
-    neigh, neigh_other = rows_of_core(w_neigh, my_core), rows_of_core(w_neigh, 1 - my_core)
-    column_blocks, base, local_part, neigh, neigh_other = lax.optimization_barrier(
-        (column_blocks, base, local_part, neigh, neigh_other)
+    quarter = (X, rows // X, columns)
+    mine_f = lax.all_to_all(features.reshape(quarter), "x", 0, 0, tiled=True)
+    other_f = swap_cores(mine_f)
+    base = jnp.broadcast_to(bias_row.astype(jnp.float32), quarter)
+    base = add_product(base, mine_f, rows_of_core(root, my_core))
+    base = add_product(base, other_f, rows_of_core(root, 1 - my_core))
+    neigh_mine, neigh_other = rows_of_core(neigh, my_core), rows_of_core(neigh, 1 - my_core)
+    column_blocks, base, local_part, neigh_mine, neigh_other = lax.optimization_barrier(
+        (column_blocks, base, local_part, neigh_mine, neigh_other)
     )
 
-    sent, own = partial_sums(told, place, column_blocks, mine, other)
-    came = lax.all_to_all(sent.reshape(Y, rows, columns), "y", 0, 0, tiled=True)
-    total = lax.optimization_barrier(local_part + own).reshape(rows, columns)
-    for i in range(Y):
-        total = total + came[i].astype(jnp.float32)
-    mine_a = to_all(total.astype(jnp.bfloat16), "x", X)
-    other_a = swap_cores(mine_a)
-    base = add_product(base, mine_a, neigh)
-    return add_product(base, other_a, neigh_other, last=True)
+    sent = partial_sums(told, place, column_blocks, local_part, mine, other)
+    came = lax.all_to_all(sent.reshape((Y * X,) + quarter[1:]), ("y", "x"), 0, 0, tiled=True).astype(jnp.float32)
+    aggregate = sum(came[y * X : (y + 1) * X] for y in range(Y)).astype(jnp.bfloat16)
+    other_a = swap_cores(aggregate)
+    base = add_product(base, aggregate, neigh_mine)
+    out = add_product(base, other_a, neigh_other, last=True)
+    return lax.all_to_all(out, "x", 0, 0, tiled=True).reshape(rows, columns)
 
 
 def solution(mesh):

time: 143 us -> 140 us (0.979)
  starting transfers between devices: 35.1 us -> 44.7 us
  blocking collectives: 34.9 us -> 27.2 us
  waiting for transfers between devices: 21.9 us -> 15.8 us
  local copies, waits for them, and re-layouts: 11.7 us -> 13.4 us
  Pallas kernels: 16.9 us -> 15.2 us
    ppermute x0 -> x3, starting transfers between devices: none -> 11.1 us  [of_ring(): lax.ppermute(array, 'x', [(i, (i + r) % X) for i in range(X)])]
    all_gather x1, waiting for transfers between devices: 2.26 us -> 11.4 us  [body(): column_blocks = lax.all_gather(history, 'z', axis=0, tiled=True)]
    all_to_all x1, waiting for transfers between devices: 8.83 us -> 0.01 us  [to_all(): lax.all_to_all(jnp.broadcast_to(array[None], (size,) + array.shape), axis...]
    all_to_all x2, blocking collectives: 34.9 us -> 27.2 us  [the longest x1 18.4 us: body(): lax.all_to_all(sent.reshape((Y * X,) + quarter[1:]), ('y', 'x'), 0, 0, ti...]
    all_to_all x1, waiting for transfers between devices: 8.64 us -> 2.95 us  [body(): mine_f = lax.all_to_all(features.reshape(quarter), 'x', 0, 0, tiled=True)]
    another operation x2 -> x4, other arithmetic: 0.02 us -> 3.89 us  [the longest x2 3.86 us: of_ring(): return jnp.stack(came)[(x - jnp.arange(X)) % X]]
    gather x0 -> x1, local copies, waits for them, and re-layouts: none -> 3.84 us  [of_ring(): return jnp.stack(came)[(x - jnp.arange(X)) % X]]
    all_to_all x1, starting transfers between devices: 4.67 us -> 8.32 us  [body(): mine_f = lax.all_to_all(features.reshape(quarter), 'x', 0, 0, tiled=True)]
  transfers between devices with their start and end apart: 6 -> 9, of which waited for: 4 -> 3; matrix products, arithmetic and copies ran while one was open for 10% -> 13% of each run, Pallas kernels for 7% -> 7%
where the time goes in v3:
time: 140 us; the launch traced here: 139 us
  starting transfers between devices  44.7 us (32%)
  blocking collectives  27.2 us (19%)
  waiting for transfers between devices  15.8 us (11%)
  Pallas kernels  15.2 us (11%)
  between operations  13.7 us (10%)
  local copies, waits for them, and re-layouts  13.4 us (10%)
  other arithmetic  6.79 us (5%)
  matrix products  1.99 us (1%)
    ppermute x3, starting transfers between devices, swap_cores(): return lax.ppermute(array, 'core', [(0, 1), (1, 0)])  20.1 us
    all_to_all x1, blocking collectives, body(): lax.all_to_all(sent.reshape((Y * X,) + quarter[1:]), ('y', 'x'), 0, 0, ti...  18.4 us
    all_gather x1, waiting for transfers between devices, body(): column_blocks = lax.all_gather(history, 'z', axis=0, tiled=True)  11.4 us
    ppermute x3, starting transfers between devices, of_ring(): lax.ppermute(array, 'x', [(i, (i + r) % X) for i in range(X)])  11.1 us
    all_to_all x1, blocking collectives, body(): return lax.all_to_all(out, 'x', 0, 0, tiled=True).reshape(rows, columns)  8.81 us
    all_to_all x1, starting transfers between devices, body(): mine_f = lax.all_to_all(features.reshape(quarter), 'x', 0, 0, tiled=True)  8.32 us
    pallas_call x1, Pallas kernels, partial_sums(): pl.pallas_call(pick_kernel, out_shape=(jax.ShapeDtypeStruct((Y, 2 * REFS...  6.8 us
    all_to_all x1, starting transfers between devices, to_all(): lax.all_to_all(jnp.broadcast_to(array[None], (size,) + array.shape), axis...  5.14 us
  transfers between devices with their start and end apart: 9, of which 3 were waited for; matrix products, arithmetic and copies ran while one was open for 13% of the time, Pallas kernels for 7%

profile of v3, /device:TPU:1, one launch (start us, length us, event | category | flops | bytes accessed | tf_op | source)
XLA Modules:
  0.0 138.8 jit_solution(10848677276676535268)
XLA Ops:
  6.5 0.7 all-gather.2.cloned.1.call-update
  7.3 0.7 iota_compare_fusion.4
  8.1 0.8 copy.26
  8.9 0.7 fusion.10
  10.0 1.4 %broadcast_in_dim.45 = bf16[4,1552,128]{2,1,0:T(8,128)(2,1)} broadcast(bf16[1552,128]{1,0:T(8,128)(2,1)S(1)} %pad_maximum_fusion.1), dimensions={1,2} | broadcast | bytes 1986560 | tf_op jit(solution)/shard_map/broadcast_in_dim | solution.py:213
  11.4 5.1 %all-to-all-start = ((bf16[4,1552,128]{2,1,0:T(8,128)(2,1)}), bf16[4,1552,128]{2,1,0:T(8,128)(2,1)S(1)}, u32[]{:S(2)}, u32[]{:S(2)}) async-start(bf16[4,1552,128]{2,1,0:T(8,128)(2,1)} %broadcast_in_dim.45), calls=%async_computation | async-start | bytes 3178496 | tf_op jit(solution)/shard_map/all_to_all | solution.py:213
  16.5 0.9 fusion.16
  17.4 4.6 %collective-permute-start.3 = (bf16[2064,128]{1,0:T(8,128)(2,1)}, bf16[2064,128]{1,0:T(8,128)(2,1)}, u32[]{:S(2)}, u32[]{:S(2)}) collective-permute-start(bf16[2064,128]{1,0:T(8,128)(2,1)} %get-tuple-element.28), channel_id=1, source_target_pairs={{0,4},{2,6},{4,0},{6,2},{1,5},{3,7},{5,1},{7,3},{8,12},{10,14},{12... | collective-permute-start | bytes 1585160 | tf_op jit(solution)/shard_map/ppermute | solution.py:221
  22.1 2.2 %collective-permute-start.2 = (bf16[2064,128]{1,0:T(8,128)(2,1)}, bf16[2064,128]{1,0:T(8,128)(2,1)}, u32[]{:S(2)}, u32[]{:S(2)}) collective-permute-start(bf16[2064,128]{1,0:T(8,128)(2,1)} %get-tuple-element.28), channel_id=1, source_target_pairs={{0,2},{2,4},{4,6},{6,0},{1,3},{3,5},{5,7},{7,1},{8,10},{10,12},{12... | collective-permute-start | bytes 1585160 | tf_op jit(solution)/shard_map/ppermute | solution.py:221
  24.3 4.3 %collective-permute-start.4 = (bf16[2064,128]{1,0:T(8,128)(2,1)}, bf16[2064,128]{1,0:T(8,128)(2,1)}, u32[]{:S(2)}, u32[]{:S(2)}) collective-permute-start(bf16[2064,128]{1,0:T(8,128)(2,1)} %get-tuple-element.28), channel_id=1, source_target_pairs={{0,6},{2,0},{4,2},{6,4},{1,7},{3,1},{5,3},{7,5},{8,14},{10,8},{12,... | collective-permute-start | bytes 1585160 | tf_op jit(solution)/shard_map/ppermute | solution.py:221
  28.6 1.5 %gather_fusion.1 = bf16[8,128,128]{2,1,0:T(8,128)(2,1)S(1)} fusion(bf16[8,128,128]{2,1,0:T(8,128)(2,1)} %bitcast.16, s32[1024]{0:T(1024)S(1)} %pad_clamp_fusion), kind=kCustom, calls=%fused_computation.1 | custom fusion | bytes 524320 | tf_op jit(solution)/shard_map/gather | solution.py:262
  30.2 2.0 %convolution_bitcast_fusion.local = f32[8,128,128]{2,1,0:T(8,128)} fusion(bf16[8,128,128]{2,1,0:T(8,128)(2,1)} %param.17, bf16[8,128,128]{2,1,0:T(8,128)(2,1)S(1)} %gather_fusion.1), kind=kOutput, calls=%fused_computation.3 | convolution fusion | flops 33554432 | bytes 1048576 | tf_op jit(solution)/shard_map/bij,bjc->bic/dot_general | solution.py:263
  32.2 8.3 %all-to-all-start.1 = ((bf16[4,256,128]{2,1,0:T(8,128)(2,1)}), bf16[4,256,128]{2,1,0:T(8,128)(2,1)}, u32[]{:S(2)}, u32[]{:S(2)}) async-start(bf16[4,256,128]{2,1,0:T(8,128)(2,1)} %bitcast.5), calls=%async_computation.1 | async-start | bytes 524288 | tf_op jit(solution)/shard_map/all_to_all | solution.py:265
  40.5 4.1 %collective-permute-start = (bf16[4,1552,128]{2,1,0:T(8,128)(2,1)S(1)}, bf16[4,1552,128]{2,1,0:T(8,128)(2,1)}, u32[]{:S(2)}, u32[]{:S(2)}) collective-permute-start(bf16[4,1552,128]{2,1,0:T(8,128)(2,1)S(1)} %all-to-all-done.mine), channel_id=1, source_target_pairs={{0,1},{1,0},{2,3},{3,2},{4,5},{5,4},{6,7},{7,6},{8,9},{9,8},{10,11... | collective-permute-start | bytes 4767752 | tf_op jit(solution)/shard_map/ppermute | solution.py:217
  44.7 3.0 %all-to-all-done.1.parts = bf16[4,256,128]{2,1,0:T(8,128)(2,1)} async-done(((bf16[4,256,128]{2,1,0:T(8,128)(2,1)}), bf16[4,256,128]{2,1,0:T(8,128)(2,1)}, u32[]{:S(2)}, u32[]{:S(2)}) %all-to-all-start.1) | async-done | bytes 262176 | tf_op jit(solution)/shard_map/all_to_all | solution.py:265
  47.6 4.0 %collective-permute-start.1 = (bf16[4,256,128]{2,1,0:T(8,128)(2,1)}, bf16[4,256,128]{2,1,0:T(8,128)(2,1)}, u32[]{:S(2)}, u32[]{:S(2)}) collective-permute-start(bf16[4,256,128]{2,1,0:T(8,128)(2,1)} %all-to-all-done.1.parts), channel_id=1, source_target_pairs={{0,1},{1,0},{2,3},{3,2},{4,5},{5,4},{6,7},{7,6},{8,9},{9,8},{10,11... | collective-permute-start | bytes 786440 | tf_op jit(solution)/shard_map/ppermute | solution.py:217
  51.6 3.0 %pad_maximum_fusion = bf16[4,2064,128]{2,1,0:T(8,128)(2,1)} fusion(bf16[1,2064,128]{2,1,0:T(8,128)(2,1)} %bitcast.10, bf16[1,2064,128]{2,1,0:T(8,128)(2,1)} %bitcast.9, bf16[1,2064,128]{2,1,0:T(8,128)(2,1)} %bitcast.8, bf16[1,2064,128]{2,1,0:T(8,128)(2,1)S(1)} %get-tuple-element.27), kind=kLoop, calls=%fused_computation.2 | loop fusion | flops 3170304 | bytes 4227072 | tf_op jit(solution)/shard_map/stack | solution.py:222
  54.6 3.8 %gather_fusion = bf16[4,2064,128]{2,1,0:T(8,128)(2,1)} fusion(bf16[4,2064,128]{2,1,0:T(8,128)(2,1)} %pad_maximum_fusion, s32[1024]{0:T(1024)S(1)} %pad_clamp_fusion.1), kind=kCustom, calls=%fused_computation | custom fusion | bytes 4227088 | tf_op jit(solution)/shard_map/gather | solution.py:222
  58.4 1.7 %fusion.17 = (bf16[4,1024,128]{2,1,0:T(8,128)(2,1)S(1)}, bf16[4,1024,128]{2,1,0:T(8,128)(2,1)S(1)}) fusion(bf16[4,2064,128]{2,1,0:T(8,128)(2,1)} %gather_fusion), kind=kLoop, calls=%fused_computation.59 | loop fusion | bytes 4194304 | tf_op jit(solution)/shard_map/slice | solution.py:247
  60.3 0.7 slice_convert_fusion
  61.1 1.4 add_product.4.base
  62.5 1.4 add_product.5.base
  63.9 0.8 copy-done.2
  64.7 6.8 %pick_tiles.1 = (s32[4,50]{1,0:T(4,128)S(1)}, bf16[4,24,128,128]{3,2,1,0:T(8,128)(2,1)S(1)}) custom-call(s32[4,48]{1,0:T(4,128)S(1)} %reshape.218.notes, s32[2]{0:T(128)S(1)} %pad_add_fusion.place, bf16[4,1552,128]{2,1,0:T(8,128)(2,1)S(1)} %all-to-all-done.mine, bf16[4,1552,128]{2,1,0:T(8,128)(2,1)} %collective-permute-done.other), custom_call_target="tpu_custom_call" | custom-call | bytes 4194304 | tf_op jit(solution)/shard_map/pick_tiles/pallas_call | solution.py:147
  71.6 1.7 %copy-done.1 = bf16[4,24,128,128]{3,2,1,0:T(8,128)(2,1)} copy-done((bf16[4,24,128,128]{3,2,1,0:T(8,128)(2,1)}, bf16[4,24,128,128]{3,2,1,0:T(8,128)(2,1)S(1)}, u32[]{:S(2)}) %copy-start.1) | copy-done | bytes 3145752
  73.8 11.4 %all-gather.2.cloned.1.call-done.blocks = bf16[16384,128]{1,0:T(8,128)(2,1)} async-done(((bf16[1024,128]{1,0:T(8,128)(2,1)}), bf16[16384,128]{1,0:T(8,128)(2,1)}) %all-gather.2.cloned.1.call-update) | async-done | bytes 4194320 | tf_op jit(solution)/shard_map/all_gather | solution.py:242
  85.3 4.7 %partial_sums.1 = bf16[32,128,128]{2,1,0:T(8,128)(2,1)} custom-call(s32[4,50]{1,0:T(4,128)} %copy-done.4, bf16[16384,128]{1,0:T(8,128)(2,1)} %all-gather.2.cloned.1.call-done.blocks, bf16[4,24,128,128]{3,2,1,0:T(8,128)(2,1)} %copy-done.1, f32[8,128,128]{2,1,0:T(8,128)} %convolution_bitcast_fusion.local), custom_call_target="tpu_custom_call" | custom-call | flops 100663296 | bytes 4194304 | tf_op jit(solution)/shard_map/partial_sums/pallas_call | solution.py:164
  90.0 18.4 %all_to_all.20 = bf16[16,256,128]{2,1,0:T(8,128)(2,1)S(1)} all-to-all(bf16[16,256,128]{2,1,0:T(8,128)(2,1)} %bitcast.64), channel_id=1, replica_groups=mesh['z'=16,'y'=4,'x'=4,'core'=2] {'y','x'}, dimensions={0} | all-to-all | bytes 2097152 | tf_op jit(solution)/shard_map/all_to_all | solution.py:276
  108.8 12.1 %collective-permute-start.5 = (bf16[4,256,128]{2,1,0:T(8,128)(2,1)S(1)}, bf16[4,256,128]{2,1,0:T(8,128)(2,1)S(1)}, u32[]{:S(2)}, u32[]{:S(2)}) collective-permute-start(bf16[4,256,128]{2,1,0:T(8,128)(2,1)S(1)} %fusion.2.parts), channel_id=1, source_target_pairs={{0,1},{1,0},{2,3},{3,2},{4,5},{5,4},{6,7},{7,6},{8,9},{9,8},{10,11... | collective-permute-start | bytes 786440 | tf_op jit(solution)/shard_map/ppermute | solution.py:217
  121.3 0.7 collective-permute-done.5.parts
  122.4 8.8 %all_to_all.21 = bf16[4,256,128]{2,1,0:T(8,128)(2,1)S(1)} all-to-all(bf16[4,256,128]{2,1,0:T(8,128)(2,1)S(1)} %add_product.7), channel_id=1, replica_groups=mesh['z'=16,'y'=4,'x'=4,'core'=2] {'x'}, dimensions={0} | all-to-all | bytes 524288 | tf_op jit(solution)/shard_map/all_to_all | solution.py:281
  131.2 0.7 copy.40
  (44 shorter events, 2.6 us)
Async XLA Ops:
  6.5 3.3 %copy-start = (bf16[8,3,128,128]{3,2,1,0:T(8,128)(2,1)S(1)}, bf16[8,3,128,128]{3,2,1,0:T(8,128)(2,1)}, u32[]{:S(2)}) copy-start(bf16[8,3,128,128]{3,2,1,0:T(8,128)(2,1)} %param.18) | copy-start | bytes 2359300
  6.5 78.7 %all-gather.2.cloned.1.call-start = ((), (), s32[]{:S(2)}) async-start(), calls=%async_computation.4 | async-start | bytes 4456448 | tf_op jit(solution)/shard_map/all_gather | solution.py:242
  9.9 6.6 %copy-start.5 = (bf16[1024,128]{1,0:T(8,128)(2,1)S(1)}, bf16[1024,128]{1,0:T(8,128)(2,1)}, u32[]{:S(2)}) copy-start(bf16[1024,128]{1,0:T(8,128)(2,1)} %param.15) | copy-start | bytes 786436
  9.9 6.6 %copy-start.6 = (bf16[1024,128]{1,0:T(8,128)(2,1)S(1)}, bf16[1024,128]{1,0:T(8,128)(2,1)}, u32[]{:S(2)}) copy-start(bf16[1024,128]{1,0:T(8,128)(2,1)} %param.14) | copy-start | bytes 786436
  10.0 6.6 %copy-start.7 = (bf16[128]{0:T(256)(128)(2,1)S(1)}, bf16[128]{0:T(256)(128)(2,1)}, u32[]{:S(2)}) copy-start(bf16[128]{0:T(256)(128)(2,1)} %param.16) | copy-start | bytes 772
  11.4 17.2 %copy-start.8 = (s32[8]{0:T(128)S(1)}, s32[8]{0:T(128)}, u32[]{:S(2)}) copy-start(s32[8]{0:T(128)} %param.19) | copy-start | bytes 100
  11.4 20.8 %all-to-all-start = ((bf16[4,1552,128]{2,1,0:T(8,128)(2,1)}), bf16[4,1552,128]{2,1,0:T(8,128)(2,1)S(1)}, u32[]{:S(2)}, u32[]{:S(2)}) async-start(bf16[4,1552,128]{2,1,0:T(8,128)(2,1)} %broadcast_in_dim.45), calls=%async_computation | async-start | bytes 3178496 | tf_op jit(solution)/shard_map/all_to_all | solution.py:213
  17.4 34.2 %collective-permute-start.3 = (bf16[2064,128]{1,0:T(8,128)(2,1)}, bf16[2064,128]{1,0:T(8,128)(2,1)}, u32[]{:S(2)}, u32[]{:S(2)}) collective-permute-start(bf16[2064,128]{1,0:T(8,128)(2,1)} %get-tuple-element.28), channel_id=1, source_target_pairs={{0,4},{2,6},{4,0},{6,2},{1,5},{3,7},{5,1},{7,3},{8,12},{10,14},{12... | collective-permute-start | bytes 1585160 | tf_op jit(solution)/shard_map/ppermute | solution.py:221
  22.1 29.5 %collective-permute-start.2 = (bf16[2064,128]{1,0:T(8,128)(2,1)}, bf16[2064,128]{1,0:T(8,128)(2,1)}, u32[]{:S(2)}, u32[]{:S(2)}) collective-permute-start(bf16[2064,128]{1,0:T(8,128)(2,1)} %get-tuple-element.28), channel_id=1, source_target_pairs={{0,2},{2,4},{4,6},{6,0},{1,3},{3,5},{5,7},{7,1},{8,10},{10,12},{12... | collective-permute-start | bytes 1585160 | tf_op jit(solution)/shard_map/ppermute | solution.py:221
  24.3 27.3 %collective-permute-start.4 = (bf16[2064,128]{1,0:T(8,128)(2,1)}, bf16[2064,128]{1,0:T(8,128)(2,1)}, u32[]{:S(2)}, u32[]{:S(2)}) collective-permute-start(bf16[2064,128]{1,0:T(8,128)(2,1)} %get-tuple-element.28), channel_id=1, source_target_pairs={{0,6},{2,0},{4,2},{6,4},{1,7},{3,1},{5,3},{7,5},{8,14},{10,8},{12,... | collective-permute-start | bytes 1585160 | tf_op jit(solution)/shard_map/ppermute | solution.py:221
  32.2 15.4 %all-to-all-start.1 = ((bf16[4,256,128]{2,1,0:T(8,128)(2,1)}), bf16[4,256,128]{2,1,0:T(8,128)(2,1)}, u32[]{:S(2)}, u32[]{:S(2)}) async-start(bf16[4,256,128]{2,1,0:T(8,128)(2,1)} %bitcast.5), calls=%async_computation.1 | async-start | bytes 524288 | tf_op jit(solution)/shard_map/all_to_all | solution.py:265
  40.5 24.2 %collective-permute-start = (bf16[4,1552,128]{2,1,0:T(8,128)(2,1)S(1)}, bf16[4,1552,128]{2,1,0:T(8,128)(2,1)}, u32[]{:S(2)}, u32[]{:S(2)}) collective-permute-start(bf16[4,1552,128]{2,1,0:T(8,128)(2,1)S(1)} %all-to-all-done.mine), channel_id=1, source_target_pairs={{0,1},{1,0},{2,3},{3,2},{4,5},{5,4},{6,7},{7,6},{8,9},{9,8},{10,11... | collective-permute-start | bytes 4767752 | tf_op jit(solution)/shard_map/ppermute | solution.py:217
  47.6 14.8 %collective-permute-start.1 = (bf16[4,256,128]{2,1,0:T(8,128)(2,1)}, bf16[4,256,128]{2,1,0:T(8,128)(2,1)}, u32[]{:S(2)}, u32[]{:S(2)}) collective-permute-start(bf16[4,256,128]{2,1,0:T(8,128)(2,1)} %all-to-all-done.1.parts), channel_id=1, source_target_pairs={{0,1},{1,0},{2,3},{3,2},{4,5},{5,4},{6,7},{7,6},{8,9},{9,8},{10,11... | collective-permute-start | bytes 786440 | tf_op jit(solution)/shard_map/ppermute | solution.py:217
  63.8 0.8 copy-start.2
  71.5 1.7 %copy-start.1 = (bf16[4,24,128,128]{3,2,1,0:T(8,128)(2,1)}, bf16[4,24,128,128]{3,2,1,0:T(8,128)(2,1)S(1)}, u32[]{:S(2)}) copy-start(bf16[4,24,128,128]{3,2,1,0:T(8,128)(2,1)S(1)} %get-tuple-element.14.tiles) | copy-start | bytes 9437188
  73.2 0.6 copy-start.4
  108.4 12.4 %copy-start.3 = (f32[4,256,128]{2,1,0:T(8,128)S(1)}, f32[4,256,128]{2,1,0:T(8,128)}, u32[]{:S(2)}) copy-start(f32[4,256,128]{2,1,0:T(8,128)} %copy-done.2) | copy-start | bytes 1572868
  108.8 13.2 %collective-permute-start.5 = (bf16[4,256,128]{2,1,0:T(8,128)(2,1)S(1)}, bf16[4,256,128]{2,1,0:T(8,128)(2,1)S(1)}, u32[]{:S(2)}, u32[]{:S(2)}) collective-permute-start(bf16[4,256,128]{2,1,0:T(8,128)(2,1)S(1)} %fusion.2.parts), channel_id=1, source_target_pairs={{0,1},{1,0},{2,3},{3,2},{4,5},{5,4},{6,7},{7,6},{8,9},{9,8},{10,11... | collective-permute-start | bytes 786440 | tf_op jit(solution)/shard_map/ppermute | solution.py:217
Sparse Core Ops, SparseCore 0:
  9.4 75.7 all-gather.1

commit v4 on v3

--- a/solution.py
+++ b/solution.py
@@ -79,7 +79,7 @@
 
 
 def partial_kernel(
-    table, blocks, tiles, local, sent, block_buf, tile_buf, local_buf, sent_buf, total, block_sem, tile_sem, out_sem
+    table, blocks, tiles, local, sent, block_buf, tile_buf, local_buf, total, block_sem, tile_sem, local_sem
 ):
     count = [table[peer, 2 * REFS] for peer in range(Y)]
     me = table[0, 2 * REFS + 1]
@@ -107,10 +107,9 @@
                 def _():
                     block_copy(peer, i).start()
 
-    local_copy = pltpu.make_async_copy(local, local_buf, out_sem.at[Y])
+    local_copy = pltpu.make_async_copy(local, local_buf, local_sem)
     local_copy.start()
     total[...] = jnp.zeros_like(total)
-    copies = []
     for peer in range(Y):
 
         @pl.loop(0, groups(peer))
@@ -135,11 +134,7 @@
             total[pl.ds(peer * TB, TB)] += local_buf[...]
 
         at = pl.ds(peer * TB, TB)
-        sent_buf[at] = total[at].astype(sent.dtype)
-        copies.append(pltpu.make_async_copy(sent_buf.at[at], sent.at[at], out_sem.at[peer]))
-        copies[-1].start()
-    for copy in copies:
-        copy.wait()
+        sent[at] = total[at].astype(sent.dtype)
 
 
 def partial_sums(notes, place, blocks, local, mine, other):
@@ -165,16 +160,15 @@
         partial_kernel,
         out_shape=jax.ShapeDtypeStruct((Y * TB, BLK, BLK), jnp.bfloat16),
         in_specs=[smem] + [hbm] * 3,
-        out_specs=hbm,
+        out_specs=pl.BlockSpec(memory_space=pltpu.VMEM),
         scratch_shapes=[
             pltpu.VMEM((Y, REFS, BLK, BLK), jnp.bfloat16),
             pltpu.VMEM((Y, REFS, BLK, BLK), jnp.bfloat16),
             pltpu.VMEM((TB, BLK, BLK), jnp.float32),
-            pltpu.VMEM((Y * TB, BLK, BLK), jnp.bfloat16),
             pltpu.VMEM((Y * TB + 1, BLK, BLK), jnp.float32),
             pltpu.SemaphoreType.DMA((Y, REFS)),
             pltpu.SemaphoreType.DMA((Y, REFS // GROUP)),
-            pltpu.SemaphoreType.DMA((Y + 1,)),
+            pltpu.SemaphoreType.DMA,
         ],
         compiler_params=pltpu.CompilerParams(vmem_limit_bytes=60 * 1024 * 1024),
         cost_estimate=pl.CostEstimate(flops=REFS * 2 * BLK**3, bytes_accessed=4 * 2**20, transcendentals=0),

time: 140 us -> 140 us (level)
  no operation moved by 1% of the time
where the time goes in v4:
time: 140 us; the launch traced here: 139 us
  starting transfers between devices  44.6 us (32%)
  blocking collectives  27 us (19%)
  Pallas kernels  16.3 us (12%)
  waiting for transfers between devices  15.5 us (11%)
  between operations  13.7 us (10%)
  local copies, waits for them, and re-layouts  13.4 us (10%)
  other arithmetic  6.79 us (5%)
  matrix products  1.99 us (1%)
    ppermute x3, starting transfers between devices, swap_cores(): return lax.ppermute(array, 'core', [(0, 1), (1, 0)])  20 us
    all_to_all x1, blocking collectives, body(): lax.all_to_all(sent.reshape((Y * X,) + quarter[1:]), ('y', 'x'), 0, 0, ti...  18.2 us
    ppermute x3, starting transfers between devices, of_ring(): lax.ppermute(array, 'x', [(i, (i + r) % X) for i in range(X)])  11.1 us
    all_gather x1, waiting for transfers between devices, body(): column_blocks = lax.all_gather(history, 'z', axis=0, tiled=True)  11.1 us
    all_to_all x1, blocking collectives, body(): return lax.all_to_all(out, 'x', 0, 0, tiled=True).reshape(rows, columns)  8.81 us
    all_to_all x1, starting transfers between devices, body(): mine_f = lax.all_to_all(features.reshape(quarter), 'x', 0, 0, tiled=True)  8.32 us
    pallas_call x1, Pallas kernels, partial_sums(): pl.pallas_call(pick_kernel, out_shape=(jax.ShapeDtypeStruct((Y, 2 * REFS...  7.13 us
    pallas_call x1, Pallas kernels, partial_sums(): pl.pallas_call(partial_kernel, out_shape=jax.ShapeDtypeStruct((Y * TB, BL...  5.54 us
  transfers between devices with their start and end apart: 9, of which 3 were waited for; matrix products, arithmetic and copies ran while one was open for 13% of the time, Pallas kernels for 7%

profile of v4, /device:TPU:1, one launch (start us, length us, event | category | flops | bytes accessed | tf_op | source)
XLA Modules:
  0.0 139.2 jit_solution(3225757607822778591)
XLA Ops:
  6.5 0.7 all-gather.2.cloned.1.call-update
  7.3 0.7 iota_compare_fusion.4
  8.1 0.8 copy.26
  8.9 0.7 fusion.10
  10.0 1.4 %broadcast_in_dim.45 = bf16[4,1552,128]{2,1,0:T(8,128)(2,1)} broadcast(bf16[1552,128]{1,0:T(8,128)(2,1)S(1)} %pad_maximum_fusion.1), dimensions={1,2} | broadcast | bytes 1986560 | tf_op jit(solution)/shard_map/broadcast_in_dim | solution.py:207
  11.4 5.1 %all-to-all-start = ((bf16[4,1552,128]{2,1,0:T(8,128)(2,1)}), bf16[4,1552,128]{2,1,0:T(8,128)(2,1)S(1)}, u32[]{:S(2)}, u32[]{:S(2)}) async-start(bf16[4,1552,128]{2,1,0:T(8,128)(2,1)} %broadcast_in_dim.45), calls=%async_computation | async-start | bytes 3178496 | tf_op jit(solution)/shard_map/all_to_all | solution.py:207
  16.5 0.9 fusion.16
  17.4 4.6 %collective-permute-start.3 = (bf16[2064,128]{1,0:T(8,128)(2,1)}, bf16[2064,128]{1,0:T(8,128)(2,1)}, u32[]{:S(2)}, u32[]{:S(2)}) collective-permute-start(bf16[2064,128]{1,0:T(8,128)(2,1)} %get-tuple-element.28), channel_id=1, source_target_pairs={{0,4},{2,6},{4,0},{6,2},{1,5},{3,7},{5,1},{7,3},{8,12},{10,14},{12... | collective-permute-start | bytes 1585160 | tf_op jit(solution)/shard_map/ppermute | solution.py:215
  22.1 2.2 %collective-permute-start.2 = (bf16[2064,128]{1,0:T(8,128)(2,1)}, bf16[2064,128]{1,0:T(8,128)(2,1)}, u32[]{:S(2)}, u32[]{:S(2)}) collective-permute-start(bf16[2064,128]{1,0:T(8,128)(2,1)} %get-tuple-element.28), channel_id=1, source_target_pairs={{0,2},{2,4},{4,6},{6,0},{1,3},{3,5},{5,7},{7,1},{8,10},{10,12},{12... | collective-permute-start | bytes 1585160 | tf_op jit(solution)/shard_map/ppermute | solution.py:215
  24.3 4.3 %collective-permute-start.4 = (bf16[2064,128]{1,0:T(8,128)(2,1)}, bf16[2064,128]{1,0:T(8,128)(2,1)}, u32[]{:S(2)}, u32[]{:S(2)}) collective-permute-start(bf16[2064,128]{1,0:T(8,128)(2,1)} %get-tuple-element.28), channel_id=1, source_target_pairs={{0,6},{2,0},{4,2},{6,4},{1,7},{3,1},{5,3},{7,5},{8,14},{10,8},{12,... | collective-permute-start | bytes 1585160 | tf_op jit(solution)/shard_map/ppermute | solution.py:215
  28.6 1.5 %gather_fusion.1 = bf16[8,128,128]{2,1,0:T(8,128)(2,1)S(1)} fusion(bf16[8,128,128]{2,1,0:T(8,128)(2,1)} %bitcast.16, s32[1024]{0:T(1024)S(1)} %pad_clamp_fusion), kind=kCustom, calls=%fused_computation.1 | custom fusion | bytes 524320 | tf_op jit(solution)/shard_map/gather | solution.py:256
  30.2 2.0 %convolution_bitcast_fusion.local = f32[8,128,128]{2,1,0:T(8,128)} fusion(bf16[8,128,128]{2,1,0:T(8,128)(2,1)} %param.17, bf16[8,128,128]{2,1,0:T(8,128)(2,1)S(1)} %gather_fusion.1), kind=kOutput, calls=%fused_computation.3 | convolution fusion | flops 33554432 | bytes 1048576 | tf_op jit(solution)/shard_map/bij,bjc->bic/dot_general | solution.py:257
  32.2 8.3 %all-to-all-start.1 = ((bf16[4,256,128]{2,1,0:T(8,128)(2,1)}), bf16[4,256,128]{2,1,0:T(8,128)(2,1)}, u32[]{:S(2)}, u32[]{:S(2)}) async-start(bf16[4,256,128]{2,1,0:T(8,128)(2,1)} %bitcast.5), calls=%async_computation.1 | async-start | bytes 524288 | tf_op jit(solution)/shard_map/all_to_all | solution.py:259
  40.5 4.1 %collective-permute-start = (bf16[4,1552,128]{2,1,0:T(8,128)(2,1)S(1)}, bf16[4,1552,128]{2,1,0:T(8,128)(2,1)}, u32[]{:S(2)}, u32[]{:S(2)}) collective-permute-start(bf16[4,1552,128]{2,1,0:T(8,128)(2,1)S(1)} %all-to-all-done.mine), channel_id=1, source_target_pairs={{0,1},{1,0},{2,3},{3,2},{4,5},{5,4},{6,7},{7,6},{8,9},{9,8},{10,11... | collective-permute-start | bytes 4767752 | tf_op jit(solution)/shard_map/ppermute | solution.py:211
  44.7 3.0 %all-to-all-done.1.parts = bf16[4,256,128]{2,1,0:T(8,128)(2,1)} async-done(((bf16[4,256,128]{2,1,0:T(8,128)(2,1)}), bf16[4,256,128]{2,1,0:T(8,128)(2,1)}, u32[]{:S(2)}, u32[]{:S(2)}) %all-to-all-start.1) | async-done | bytes 262176 | tf_op jit(solution)/shard_map/all_to_all | solution.py:259
  47.6 4.0 %collective-permute-start.1 = (bf16[4,256,128]{2,1,0:T(8,128)(2,1)}, bf16[4,256,128]{2,1,0:T(8,128)(2,1)}, u32[]{:S(2)}, u32[]{:S(2)}) collective-permute-start(bf16[4,256,128]{2,1,0:T(8,128)(2,1)} %all-to-all-done.1.parts), channel_id=1, source_target_pairs={{0,1},{1,0},{2,3},{3,2},{4,5},{5,4},{6,7},{7,6},{8,9},{9,8},{10,11... | collective-permute-start | bytes 786440 | tf_op jit(solution)/shard_map/ppermute | solution.py:211
  51.6 3.0 %pad_maximum_fusion = bf16[4,2064,128]{2,1,0:T(8,128)(2,1)} fusion(bf16[1,2064,128]{2,1,0:T(8,128)(2,1)} %bitcast.10, bf16[1,2064,128]{2,1,0:T(8,128)(2,1)} %bitcast.9, bf16[1,2064,128]{2,1,0:T(8,128)(2,1)} %bitcast.8, bf16[1,2064,128]{2,1,0:T(8,128)(2,1)S(1)} %get-tuple-element.27), kind=kLoop, calls=%fused_computation.2 | loop fusion | flops 3170304 | bytes 4227072 | tf_op jit(solution)/shard_map/stack | solution.py:216
  54.6 3.8 %gather_fusion = bf16[4,2064,128]{2,1,0:T(8,128)(2,1)} fusion(bf16[4,2064,128]{2,1,0:T(8,128)(2,1)} %pad_maximum_fusion, s32[1024]{0:T(1024)S(1)} %pad_clamp_fusion.1), kind=kCustom, calls=%fused_computation | custom fusion | bytes 4227088 | tf_op jit(solution)/shard_map/gather | solution.py:216
  58.4 1.7 %fusion.17 = (bf16[4,1024,128]{2,1,0:T(8,128)(2,1)S(1)}, bf16[4,1024,128]{2,1,0:T(8,128)(2,1)S(1)}) fusion(bf16[4,2064,128]{2,1,0:T(8,128)(2,1)} %gather_fusion), kind=kLoop, calls=%fused_computation.59 | loop fusion | bytes 4194304 | tf_op jit(solution)/shard_map/slice | solution.py:241
  60.3 0.7 slice_convert_fusion
  61.1 1.4 add_product.4.base
  62.5 1.4 add_product.5.base
  63.9 0.8 copy-done.2
  64.7 7.1 %pick_tiles.1 = (s32[4,50]{1,0:T(4,128)S(1)}, bf16[4,24,128,128]{3,2,1,0:T(8,128)(2,1)S(1)}) custom-call(s32[4,48]{1,0:T(4,128)S(1)} %reshape.218.notes, s32[2]{0:T(128)S(1)} %pad_add_fusion.place, bf16[4,1552,128]{2,1,0:T(8,128)(2,1)S(1)} %all-to-all-done.mine, bf16[4,1552,128]{2,1,0:T(8,128)(2,1)} %collective-permute-done.other), custom_call_target="tpu_custom_call" | custom-call | bytes 4194304 | tf_op jit(solution)/shard_map/pick_tiles/pallas_call | solution.py:142
  71.9 1.7 %copy-done.1 = bf16[4,24,128,128]{3,2,1,0:T(8,128)(2,1)} copy-done((bf16[4,24,128,128]{3,2,1,0:T(8,128)(2,1)}, bf16[4,24,128,128]{3,2,1,0:T(8,128)(2,1)S(1)}, u32[]{:S(2)}) %copy-start.1) | copy-done | bytes 3145752
  74.2 11.1 %all-gather.2.cloned.1.call-done.blocks = bf16[16384,128]{1,0:T(8,128)(2,1)} async-done(((bf16[1024,128]{1,0:T(8,128)(2,1)}), bf16[16384,128]{1,0:T(8,128)(2,1)}) %all-gather.2.cloned.1.call-update) | async-done | bytes 4194320 | tf_op jit(solution)/shard_map/all_gather | solution.py:236
  85.3 5.5 %partial_sums.1 = bf16[32,128,128]{2,1,0:T(8,128)(2,1)} custom-call(s32[4,50]{1,0:T(4,128)} %copy-done.4, bf16[16384,128]{1,0:T(8,128)(2,1)} %all-gather.2.cloned.1.call-done.blocks, bf16[4,24,128,128]{3,2,1,0:T(8,128)(2,1)} %copy-done.1, f32[8,128,128]{2,1,0:T(8,128)} %convolution_bitcast_fusion.local), custom_call_target="tpu_custom_call" | custom-call | flops 100663296 | bytes 4194304 | tf_op jit(solution)/shard_map/partial_sums/pallas_call | solution.py:159
  90.8 18.2 %all_to_all.20 = bf16[16,256,128]{2,1,0:T(8,128)(2,1)S(1)} all-to-all(bf16[16,256,128]{2,1,0:T(8,128)(2,1)} %bitcast.64), channel_id=1, replica_groups=mesh['z'=16,'y'=4,'x'=4,'core'=2] {'y','x'}, dimensions={0} | all-to-all | bytes 2097152 | tf_op jit(solution)/shard_map/all_to_all | solution.py:270
  109.3 12.0 %collective-permute-start.5 = (bf16[4,256,128]{2,1,0:T(8,128)(2,1)S(1)}, bf16[4,256,128]{2,1,0:T(8,128)(2,1)S(1)}, u32[]{:S(2)}, u32[]{:S(2)}) collective-permute-start(bf16[4,256,128]{2,1,0:T(8,128)(2,1)S(1)} %fusion.2.parts), channel_id=1, source_target_pairs={{0,1},{1,0},{2,3},{3,2},{4,5},{5,4},{6,7},{7,6},{8,9},{9,8},{10,11... | collective-permute-start | bytes 786440 | tf_op jit(solution)/shard_map/ppermute | solution.py:211
  121.8 0.7 collective-permute-done.5.parts
  122.9 8.8 %all_to_all.21 = bf16[4,256,128]{2,1,0:T(8,128)(2,1)S(1)} all-to-all(bf16[4,256,128]{2,1,0:T(8,128)(2,1)S(1)} %add_product.7), channel_id=1, replica_groups=mesh['z'=16,'y'=4,'x'=4,'core'=2] {'x'}, dimensions={0} | all-to-all | bytes 524288 | tf_op jit(solution)/shard_map/all_to_all | solution.py:275
  131.7 0.7 copy.40
  (44 shorter events, 2.6 us)
Async XLA Ops:
  6.5 3.3 %copy-start = (bf16[8,3,128,128]{3,2,1,0:T(8,128)(2,1)S(1)}, bf16[8,3,128,128]{3,2,1,0:T(8,128)(2,1)}, u32[]{:S(2)}) copy-start(bf16[8,3,128,128]{3,2,1,0:T(8,128)(2,1)} %param.18) | copy-start | bytes 2359300
  6.5 78.7 %all-gather.2.cloned.1.call-start = ((), (), s32[]{:S(2)}) async-start(), calls=%async_computation.4 | async-start | bytes 4456448 | tf_op jit(solution)/shard_map/all_gather | solution.py:236
  9.9 6.6 %copy-start.5 = (bf16[1024,128]{1,0:T(8,128)(2,1)S(1)}, bf16[1024,128]{1,0:T(8,128)(2,1)}, u32[]{:S(2)}) copy-start(bf16[1024,128]{1,0:T(8,128)(2,1)} %param.15) | copy-start | bytes 786436
  9.9 6.6 %copy-start.6 = (bf16[1024,128]{1,0:T(8,128)(2,1)S(1)}, bf16[1024,128]{1,0:T(8,128)(2,1)}, u32[]{:S(2)}) copy-start(bf16[1024,128]{1,0:T(8,128)(2,1)} %param.14) | copy-start | bytes 786436
  10.0 6.6 %copy-start.7 = (bf16[128]{0:T(256)(128)(2,1)S(1)}, bf16[128]{0:T(256)(128)(2,1)}, u32[]{:S(2)}) copy-start(bf16[128]{0:T(256)(128)(2,1)} %param.16) | copy-start | bytes 772
  11.4 17.2 %copy-start.8 = (s32[8]{0:T(128)S(1)}, s32[8]{0:T(128)}, u32[]{:S(2)}) copy-start(s32[8]{0:T(128)} %param.19) | copy-start | bytes 100
  11.4 20.8 %all-to-all-start = ((bf16[4,1552,128]{2,1,0:T(8,128)(2,1)}), bf16[4,1552,128]{2,1,0:T(8,128)(2,1)S(1)}, u32[]{:S(2)}, u32[]{:S(2)}) async-start(bf16[4,1552,128]{2,1,0:T(8,128)(2,1)} %broadcast_in_dim.45), calls=%async_computation | async-start | bytes 3178496 | tf_op jit(solution)/shard_map/all_to_all | solution.py:207
  17.4 34.2 %collective-permute-start.3 = (bf16[2064,128]{1,0:T(8,128)(2,1)}, bf16[2064,128]{1,0:T(8,128)(2,1)}, u32[]{:S(2)}, u32[]{:S(2)}) collective-permute-start(bf16[2064,128]{1,0:T(8,128)(2,1)} %get-tuple-element.28), channel_id=1, source_target_pairs={{0,4},{2,6},{4,0},{6,2},{1,5},{3,7},{5,1},{7,3},{8,12},{10,14},{12... | collective-permute-start | bytes 1585160 | tf_op jit(solution)/shard_map/ppermute | solution.py:215
  22.1 29.5 %collective-permute-start.2 = (bf16[2064,128]{1,0:T(8,128)(2,1)}, bf16[2064,128]{1,0:T(8,128)(2,1)}, u32[]{:S(2)}, u32[]{:S(2)}) collective-permute-start(bf16[2064,128]{1,0:T(8,128)(2,1)} %get-tuple-element.28), channel_id=1, source_target_pairs={{0,2},{2,4},{4,6},{6,0},{1,3},{3,5},{5,7},{7,1},{8,10},{10,12},{12... | collective-permute-start | bytes 1585160 | tf_op jit(solution)/shard_map/ppermute | solution.py:215
  24.3 27.3 %collective-permute-start.4 = (bf16[2064,128]{1,0:T(8,128)(2,1)}, bf16[2064,128]{1,0:T(8,128)(2,1)}, u32[]{:S(2)}, u32[]{:S(2)}) collective-permute-start(bf16[2064,128]{1,0:T(8,128)(2,1)} %get-tuple-element.28), channel_id=1, source_target_pairs={{0,6},{2,0},{4,2},{6,4},{1,7},{3,1},{5,3},{7,5},{8,14},{10,8},{12,... | collective-permute-start | bytes 1585160 | tf_op jit(solution)/shard_map/ppermute | solution.py:215
  32.2 15.4 %all-to-all-start.1 = ((bf16[4,256,128]{2,1,0:T(8,128)(2,1)}), bf16[4,256,128]{2,1,0:T(8,128)(2,1)}, u32[]{:S(2)}, u32[]{:S(2)}) async-start(bf16[4,256,128]{2,1,0:T(8,128)(2,1)} %bitcast.5), calls=%async_computation.1 | async-start | bytes 524288 | tf_op jit(solution)/shard_map/all_to_all | solution.py:259
  40.5 24.2 %collective-permute-start = (bf16[4,1552,128]{2,1,0:T(8,128)(2,1)S(1)}, bf16[4,1552,128]{2,1,0:T(8,128)(2,1)}, u32[]{:S(2)}, u32[]{:S(2)}) collective-permute-start(bf16[4,1552,128]{2,1,0:T(8,128)(2,1)S(1)} %all-to-all-done.mine), channel_id=1, source_target_pairs={{0,1},{1,0},{2,3},{3,2},{4,5},{5,4},{6,7},{7,6},{8,9},{9,8},{10,11... | collective-permute-start | bytes 4767752 | tf_op jit(solution)/shard_map/ppermute | solution.py:211
  47.6 14.8 %collective-permute-start.1 = (bf16[4,256,128]{2,1,0:T(8,128)(2,1)}, bf16[4,256,128]{2,1,0:T(8,128)(2,1)}, u32[]{:S(2)}, u32[]{:S(2)}) collective-permute-start(bf16[4,256,128]{2,1,0:T(8,128)(2,1)} %all-to-all-done.1.parts), channel_id=1, source_target_pairs={{0,1},{1,0},{2,3},{3,2},{4,5},{5,4},{6,7},{7,6},{8,9},{9,8},{10,11... | collective-permute-start | bytes 786440 | tf_op jit(solution)/shard_map/ppermute | solution.py:211
  63.8 0.8 copy-start.2
  71.9 1.7 %copy-start.1 = (bf16[4,24,128,128]{3,2,1,0:T(8,128)(2,1)}, bf16[4,24,128,128]{3,2,1,0:T(8,128)(2,1)S(1)}, u32[]{:S(2)}) copy-start(bf16[4,24,128,128]{3,2,1,0:T(8,128)(2,1)S(1)} %get-tuple-element.14.tiles) | copy-start | bytes 9437188
  73.6 0.6 copy-start.4
  109.0 12.3 %copy-start.3 = (f32[4,256,128]{2,1,0:T(8,128)S(1)}, f32[4,256,128]{2,1,0:T(8,128)}, u32[]{:S(2)}) copy-start(f32[4,256,128]{2,1,0:T(8,128)} %copy-done.2) | copy-start | bytes 1572868
  109.3 13.1 %collective-permute-start.5 = (bf16[4,256,128]{2,1,0:T(8,128)(2,1)S(1)}, bf16[4,256,128]{2,1,0:T(8,128)(2,1)S(1)}, u32[]{:S(2)}, u32[]{:S(2)}) collective-permute-start(bf16[4,256,128]{2,1,0:T(8,128)(2,1)S(1)} %fusion.2.parts), channel_id=1, source_target_pairs={{0,1},{1,0},{2,3},{3,2},{4,5},{5,4},{6,7},{7,6},{8,9},{9,8},{10,11... | collective-permute-start | bytes 786440 | tf_op jit(solution)/shard_map/ppermute | solution.py:211
Sparse Core Ops, SparseCore 0:
  9.4 75.7 all-gather.1

commit v5 on v4

--- a/solution.py
+++ b/solution.py
@@ -99,7 +99,6 @@
 
         @pl.loop(0, groups(peer))
         def _(group):
-            tile_copy(peer, group).start()
             for u in range(GROUP):
                 i = group * GROUP + u
 
@@ -107,9 +106,11 @@
                 def _():
                     block_copy(peer, i).start()
 
+            tile_copy(peer, group).start()
+
     local_copy = pltpu.make_async_copy(local, local_buf, local_sem)
     local_copy.start()
-    total[...] = jnp.zeros_like(total)
+    total[pl.ds(0, Y * TB)] = jnp.zeros((Y * TB, BLK, BLK), jnp.float32)
     for peer in range(Y):
 
         @pl.loop(0, groups(peer))

time: 140 us -> 140 us (level)
  no operation moved by 1% of the time
where the time goes in v5:
time: 140 us; the launch traced here: 139 us
  starting transfers between devices  44.7 us (32%)
  blocking collectives  27 us (19%)
  waiting for transfers between devices  15.9 us (11%)
  Pallas kernels  15.5 us (11%)
  between operations  13.7 us (10%)
  local copies, waits for them, and re-layouts  13.4 us (10%)
  other arithmetic  6.79 us (5%)
  matrix products  1.99 us (1%)
    ppermute x3, starting transfers between devices, swap_cores(): return lax.ppermute(array, 'core', [(0, 1), (1, 0)])  20.1 us
    all_to_all x1, blocking collectives, body(): lax.all_to_all(sent.reshape((Y * X,) + quarter[1:]), ('y', 'x'), 0, 0, ti...  18.2 us
    all_gather x1, waiting for transfers between devices, body(): column_blocks = lax.all_gather(history, 'z', axis=0, tiled=True)  11.6 us
    ppermute x3, starting transfers between devices, of_ring(): lax.ppermute(array, 'x', [(i, (i + r) % X) for i in range(X)])  11.1 us
    all_to_all x1, blocking collectives, body(): return lax.all_to_all(out, 'x', 0, 0, tiled=True).reshape(rows, columns)  8.8 us
    all_to_all x1, starting transfers between devices, body(): mine_f = lax.all_to_all(features.reshape(quarter), 'x', 0, 0, tiled=True)  8.32 us
    pallas_call x1, Pallas kernels, partial_sums(): pl.pallas_call(pick_kernel, out_shape=(jax.ShapeDtypeStruct((Y, 2 * REFS...  6.67 us
    pallas_call x1, Pallas kernels, partial_sums(): pl.pallas_call(partial_kernel, out_shape=jax.ShapeDtypeStruct((Y * TB, BL...  5.25 us
  transfers between devices with their start and end apart: 9, of which 3 were waited for; matrix products, arithmetic and copies ran while one was open for 13% of the time, Pallas kernels for 7%

profile of v5, /device:TPU:1, one launch (start us, length us, event | category | flops | bytes accessed | tf_op | source)
XLA Modules:
  0.0 139.0 jit_solution(8822201192976793214)
XLA Ops:
  6.5 0.7 all-gather.2.cloned.1.call-update
  7.3 0.7 iota_compare_fusion.4
  8.1 0.8 copy.26
  8.9 0.7 fusion.10
  10.0 1.4 %broadcast_in_dim.45 = bf16[4,1552,128]{2,1,0:T(8,128)(2,1)} broadcast(bf16[1552,128]{1,0:T(8,128)(2,1)S(1)} %pad_maximum_fusion.1), dimensions={1,2} | broadcast | bytes 1986560 | tf_op jit(solution)/shard_map/broadcast_in_dim | solution.py:208
  11.4 5.1 %all-to-all-start = ((bf16[4,1552,128]{2,1,0:T(8,128)(2,1)}), bf16[4,1552,128]{2,1,0:T(8,128)(2,1)S(1)}, u32[]{:S(2)}, u32[]{:S(2)}) async-start(bf16[4,1552,128]{2,1,0:T(8,128)(2,1)} %broadcast_in_dim.45), calls=%async_computation | async-start | bytes 3178496 | tf_op jit(solution)/shard_map/all_to_all | solution.py:208
  16.5 0.9 fusion.16
  17.4 4.6 %collective-permute-start.3 = (bf16[2064,128]{1,0:T(8,128)(2,1)}, bf16[2064,128]{1,0:T(8,128)(2,1)}, u32[]{:S(2)}, u32[]{:S(2)}) collective-permute-start(bf16[2064,128]{1,0:T(8,128)(2,1)} %get-tuple-element.28), channel_id=1, source_target_pairs={{0,4},{2,6},{4,0},{6,2},{1,5},{3,7},{5,1},{7,3},{8,12},{10,14},{12... | collective-permute-start | bytes 1585160 | tf_op jit(solution)/shard_map/ppermute | solution.py:216
  22.1 2.2 %collective-permute-start.2 = (bf16[2064,128]{1,0:T(8,128)(2,1)}, bf16[2064,128]{1,0:T(8,128)(2,1)}, u32[]{:S(2)}, u32[]{:S(2)}) collective-permute-start(bf16[2064,128]{1,0:T(8,128)(2,1)} %get-tuple-element.28), channel_id=1, source_target_pairs={{0,2},{2,4},{4,6},{6,0},{1,3},{3,5},{5,7},{7,1},{8,10},{10,12},{12... | collective-permute-start | bytes 1585160 | tf_op jit(solution)/shard_map/ppermute | solution.py:216
  24.3 4.3 %collective-permute-start.4 = (bf16[2064,128]{1,0:T(8,128)(2,1)}, bf16[2064,128]{1,0:T(8,128)(2,1)}, u32[]{:S(2)}, u32[]{:S(2)}) collective-permute-start(bf16[2064,128]{1,0:T(8,128)(2,1)} %get-tuple-element.28), channel_id=1, source_target_pairs={{0,6},{2,0},{4,2},{6,4},{1,7},{3,1},{5,3},{7,5},{8,14},{10,8},{12,... | collective-permute-start | bytes 1585160 | tf_op jit(solution)/shard_map/ppermute | solution.py:216
  28.6 1.5 %gather_fusion.1 = bf16[8,128,128]{2,1,0:T(8,128)(2,1)S(1)} fusion(bf16[8,128,128]{2,1,0:T(8,128)(2,1)} %bitcast.16, s32[1024]{0:T(1024)S(1)} %pad_clamp_fusion), kind=kCustom, calls=%fused_computation.1 | custom fusion | bytes 524320 | tf_op jit(solution)/shard_map/gather | solution.py:257
  30.2 2.0 %convolution_bitcast_fusion.local = f32[8,128,128]{2,1,0:T(8,128)} fusion(bf16[8,128,128]{2,1,0:T(8,128)(2,1)} %param.17, bf16[8,128,128]{2,1,0:T(8,128)(2,1)S(1)} %gather_fusion.1), kind=kOutput, calls=%fused_computation.3 | convolution fusion | flops 33554432 | bytes 1048576 | tf_op jit(solution)/shard_map/bij,bjc->bic/dot_general | solution.py:258
  32.2 8.3 %all-to-all-start.1 = ((bf16[4,256,128]{2,1,0:T(8,128)(2,1)}), bf16[4,256,128]{2,1,0:T(8,128)(2,1)}, u32[]{:S(2)}, u32[]{:S(2)}) async-start(bf16[4,256,128]{2,1,0:T(8,128)(2,1)} %bitcast.5), calls=%async_computation.1 | async-start | bytes 524288 | tf_op jit(solution)/shard_map/all_to_all | solution.py:260
  40.5 4.1 %collective-permute-start = (bf16[4,1552,128]{2,1,0:T(8,128)(2,1)S(1)}, bf16[4,1552,128]{2,1,0:T(8,128)(2,1)}, u32[]{:S(2)}, u32[]{:S(2)}) collective-permute-start(bf16[4,1552,128]{2,1,0:T(8,128)(2,1)S(1)} %all-to-all-done.mine), channel_id=1, source_target_pairs={{0,1},{1,0},{2,3},{3,2},{4,5},{5,4},{6,7},{7,6},{8,9},{9,8},{10,11... | collective-permute-start | bytes 4767752 | tf_op jit(solution)/shard_map/ppermute | solution.py:212
  44.7 3.0 %all-to-all-done.1.parts = bf16[4,256,128]{2,1,0:T(8,128)(2,1)} async-done(((bf16[4,256,128]{2,1,0:T(8,128)(2,1)}), bf16[4,256,128]{2,1,0:T(8,128)(2,1)}, u32[]{:S(2)}, u32[]{:S(2)}) %all-to-all-start.1) | async-done | bytes 262176 | tf_op jit(solution)/shard_map/all_to_all | solution.py:260
  47.6 4.0 %collective-permute-start.1 = (bf16[4,256,128]{2,1,0:T(8,128)(2,1)}, bf16[4,256,128]{2,1,0:T(8,128)(2,1)}, u32[]{:S(2)}, u32[]{:S(2)}) collective-permute-start(bf16[4,256,128]{2,1,0:T(8,128)(2,1)} %all-to-all-done.1.parts), channel_id=1, source_target_pairs={{0,1},{1,0},{2,3},{3,2},{4,5},{5,4},{6,7},{7,6},{8,9},{9,8},{10,11... | collective-permute-start | bytes 786440 | tf_op jit(solution)/shard_map/ppermute | solution.py:212
  51.6 3.0 %pad_maximum_fusion = bf16[4,2064,128]{2,1,0:T(8,128)(2,1)} fusion(bf16[1,2064,128]{2,1,0:T(8,128)(2,1)} %bitcast.10, bf16[1,2064,128]{2,1,0:T(8,128)(2,1)} %bitcast.9, bf16[1,2064,128]{2,1,0:T(8,128)(2,1)} %bitcast.8, bf16[1,2064,128]{2,1,0:T(8,128)(2,1)S(1)} %get-tuple-element.27), kind=kLoop, calls=%fused_computation.2 | loop fusion | flops 3170304 | bytes 4227072 | tf_op jit(solution)/shard_map/stack | solution.py:217
  54.6 3.8 %gather_fusion = bf16[4,2064,128]{2,1,0:T(8,128)(2,1)} fusion(bf16[4,2064,128]{2,1,0:T(8,128)(2,1)} %pad_maximum_fusion, s32[1024]{0:T(1024)S(1)} %pad_clamp_fusion.1), kind=kCustom, calls=%fused_computation | custom fusion | bytes 4227088 | tf_op jit(solution)/shard_map/gather | solution.py:217
  58.4 1.7 %fusion.17 = (bf16[4,1024,128]{2,1,0:T(8,128)(2,1)S(1)}, bf16[4,1024,128]{2,1,0:T(8,128)(2,1)S(1)}) fusion(bf16[4,2064,128]{2,1,0:T(8,128)(2,1)} %gather_fusion), kind=kLoop, calls=%fused_computation.59 | loop fusion | bytes 4194304 | tf_op jit(solution)/shard_map/slice | solution.py:242
  60.3 0.7 slice_convert_fusion
  61.1 1.4 add_product.4.base
  62.5 1.4 add_product.5.base
  63.9 0.8 copy-done.2
  64.7 6.7 %pick_tiles.1 = (s32[4,50]{1,0:T(4,128)S(1)}, bf16[4,24,128,128]{3,2,1,0:T(8,128)(2,1)S(1)}) custom-call(s32[4,48]{1,0:T(4,128)S(1)} %reshape.218.notes, s32[2]{0:T(128)S(1)} %pad_add_fusion.place, bf16[4,1552,128]{2,1,0:T(8,128)(2,1)S(1)} %all-to-all-done.mine, bf16[4,1552,128]{2,1,0:T(8,128)(2,1)} %collective-permute-done.other), custom_call_target="tpu_custom_call" | custom-call | bytes 4194304 | tf_op jit(solution)/shard_map/pick_tiles/pallas_call | solution.py:143
  71.4 1.7 %copy-done.1 = bf16[4,24,128,128]{3,2,1,0:T(8,128)(2,1)} copy-done((bf16[4,24,128,128]{3,2,1,0:T(8,128)(2,1)}, bf16[4,24,128,128]{3,2,1,0:T(8,128)(2,1)S(1)}, u32[]{:S(2)}) %copy-start.1) | copy-done | bytes 3145752
  73.7 11.6 %all-gather.2.cloned.1.call-done.blocks = bf16[16384,128]{1,0:T(8,128)(2,1)} async-done(((bf16[1024,128]{1,0:T(8,128)(2,1)}), bf16[16384,128]{1,0:T(8,128)(2,1)}) %all-gather.2.cloned.1.call-update) | async-done | bytes 4194320 | tf_op jit(solution)/shard_map/all_gather | solution.py:237
  85.3 5.3 %partial_sums.1 = bf16[32,128,128]{2,1,0:T(8,128)(2,1)} custom-call(s32[4,50]{1,0:T(4,128)} %copy-done.4, bf16[16384,128]{1,0:T(8,128)(2,1)} %all-gather.2.cloned.1.call-done.blocks, bf16[4,24,128,128]{3,2,1,0:T(8,128)(2,1)} %copy-done.1, f32[8,128,128]{2,1,0:T(8,128)} %convolution_bitcast_fusion.local), custom_call_target="tpu_custom_call" | custom-call | flops 100663296 | bytes 4194304 | tf_op jit(solution)/shard_map/partial_sums/pallas_call | solution.py:160
  90.5 18.2 %all_to_all.20 = bf16[16,256,128]{2,1,0:T(8,128)(2,1)S(1)} all-to-all(bf16[16,256,128]{2,1,0:T(8,128)(2,1)} %bitcast.64), channel_id=1, replica_groups=mesh['z'=16,'y'=4,'x'=4,'core'=2] {'y','x'}, dimensions={0} | all-to-all | bytes 2097152 | tf_op jit(solution)/shard_map/all_to_all | solution.py:271
  109.0 12.1 %collective-permute-start.5 = (bf16[4,256,128]{2,1,0:T(8,128)(2,1)S(1)}, bf16[4,256,128]{2,1,0:T(8,128)(2,1)S(1)}, u32[]{:S(2)}, u32[]{:S(2)}) collective-permute-start(bf16[4,256,128]{2,1,0:T(8,128)(2,1)S(1)} %fusion.2.parts), channel_id=1, source_target_pairs={{0,1},{1,0},{2,3},{3,2},{4,5},{5,4},{6,7},{7,6},{8,9},{9,8},{10,11... | collective-permute-start | bytes 786440 | tf_op jit(solution)/shard_map/ppermute | solution.py:212
  121.6 0.7 collective-permute-done.5.parts
  122.7 8.8 %all_to_all.21 = bf16[4,256,128]{2,1,0:T(8,128)(2,1)S(1)} all-to-all(bf16[4,256,128]{2,1,0:T(8,128)(2,1)S(1)} %add_product.7), channel_id=1, replica_groups=mesh['z'=16,'y'=4,'x'=4,'core'=2] {'x'}, dimensions={0} | all-to-all | bytes 524288 | tf_op jit(solution)/shard_map/all_to_all | solution.py:276
  131.5 0.7 copy.40
  (44 shorter events, 2.6 us)
Async XLA Ops:
  6.5 3.3 %copy-start = (bf16[8,3,128,128]{3,2,1,0:T(8,128)(2,1)S(1)}, bf16[8,3,128,128]{3,2,1,0:T(8,128)(2,1)}, u32[]{:S(2)}) copy-start(bf16[8,3,128,128]{3,2,1,0:T(8,128)(2,1)} %param.18) | copy-start | bytes 2359300
  6.5 78.7 %all-gather.2.cloned.1.call-start = ((), (), s32[]{:S(2)}) async-start(), calls=%async_computation.4 | async-start | bytes 4456448 | tf_op jit(solution)/shard_map/all_gather | solution.py:237
  9.9 6.6 %copy-start.5 = (bf16[1024,128]{1,0:T(8,128)(2,1)S(1)}, bf16[1024,128]{1,0:T(8,128)(2,1)}, u32[]{:S(2)}) copy-start(bf16[1024,128]{1,0:T(8,128)(2,1)} %param.15) | copy-start | bytes 786436
  9.9 6.6 %copy-start.6 = (bf16[1024,128]{1,0:T(8,128)(2,1)S(1)}, bf16[1024,128]{1,0:T(8,128)(2,1)}, u32[]{:S(2)}) copy-start(bf16[1024,128]{1,0:T(8,128)(2,1)} %param.14) | copy-start | bytes 786436
  10.0 6.6 %copy-start.7 = (bf16[128]{0:T(256)(128)(2,1)S(1)}, bf16[128]{0:T(256)(128)(2,1)}, u32[]{:S(2)}) copy-start(bf16[128]{0:T(256)(128)(2,1)} %param.16) | copy-start | bytes 772
  11.4 17.2 %copy-start.8 = (s32[8]{0:T(128)S(1)}, s32[8]{0:T(128)}, u32[]{:S(2)}) copy-start(s32[8]{0:T(128)} %param.19) | copy-start | bytes 100
  11.4 20.8 %all-to-all-start = ((bf16[4,1552,128]{2,1,0:T(8,128)(2,1)}), bf16[4,1552,128]{2,1,0:T(8,128)(2,1)S(1)}, u32[]{:S(2)}, u32[]{:S(2)}) async-start(bf16[4,1552,128]{2,1,0:T(8,128)(2,1)} %broadcast_in_dim.45), calls=%async_computation | async-start | bytes 3178496 | tf_op jit(solution)/shard_map/all_to_all | solution.py:208
  17.4 34.2 %collective-permute-start.3 = (bf16[2064,128]{1,0:T(8,128)(2,1)}, bf16[2064,128]{1,0:T(8,128)(2,1)}, u32[]{:S(2)}, u32[]{:S(2)}) collective-permute-start(bf16[2064,128]{1,0:T(8,128)(2,1)} %get-tuple-element.28), channel_id=1, source_target_pairs={{0,4},{2,6},{4,0},{6,2},{1,5},{3,7},{5,1},{7,3},{8,12},{10,14},{12... | collective-permute-start | bytes 1585160 | tf_op jit(solution)/shard_map/ppermute | solution.py:216
  22.1 29.5 %collective-permute-start.2 = (bf16[2064,128]{1,0:T(8,128)(2,1)}, bf16[2064,128]{1,0:T(8,128)(2,1)}, u32[]{:S(2)}, u32[]{:S(2)}) collective-permute-start(bf16[2064,128]{1,0:T(8,128)(2,1)} %get-tuple-element.28), channel_id=1, source_target_pairs={{0,2},{2,4},{4,6},{6,0},{1,3},{3,5},{5,7},{7,1},{8,10},{10,12},{12... | collective-permute-start | bytes 1585160 | tf_op jit(solution)/shard_map/ppermute | solution.py:216
  24.3 27.3 %collective-permute-start.4 = (bf16[2064,128]{1,0:T(8,128)(2,1)}, bf16[2064,128]{1,0:T(8,128)(2,1)}, u32[]{:S(2)}, u32[]{:S(2)}) collective-permute-start(bf16[2064,128]{1,0:T(8,128)(2,1)} %get-tuple-element.28), channel_id=1, source_target_pairs={{0,6},{2,0},{4,2},{6,4},{1,7},{3,1},{5,3},{7,5},{8,14},{10,8},{12,... | collective-permute-start | bytes 1585160 | tf_op jit(solution)/shard_map/ppermute | solution.py:216
  32.2 15.4 %all-to-all-start.1 = ((bf16[4,256,128]{2,1,0:T(8,128)(2,1)}), bf16[4,256,128]{2,1,0:T(8,128)(2,1)}, u32[]{:S(2)}, u32[]{:S(2)}) async-start(bf16[4,256,128]{2,1,0:T(8,128)(2,1)} %bitcast.5), calls=%async_computation.1 | async-start | bytes 524288 | tf_op jit(solution)/shard_map/all_to_all | solution.py:260
  40.5 24.2 %collective-permute-start = (bf16[4,1552,128]{2,1,0:T(8,128)(2,1)S(1)}, bf16[4,1552,128]{2,1,0:T(8,128)(2,1)}, u32[]{:S(2)}, u32[]{:S(2)}) collective-permute-start(bf16[4,1552,128]{2,1,0:T(8,128)(2,1)S(1)} %all-to-all-done.mine), channel_id=1, source_target_pairs={{0,1},{1,0},{2,3},{3,2},{4,5},{5,4},{6,7},{7,6},{8,9},{9,8},{10,11... | collective-permute-start | bytes 4767752 | tf_op jit(solution)/shard_map/ppermute | solution.py:212
  47.6 14.8 %collective-permute-start.1 = (bf16[4,256,128]{2,1,0:T(8,128)(2,1)}, bf16[4,256,128]{2,1,0:T(8,128)(2,1)}, u32[]{:S(2)}, u32[]{:S(2)}) collective-permute-start(bf16[4,256,128]{2,1,0:T(8,128)(2,1)} %all-to-all-done.1.parts), channel_id=1, source_target_pairs={{0,1},{1,0},{2,3},{3,2},{4,5},{5,4},{6,7},{7,6},{8,9},{9,8},{10,11... | collective-permute-start | bytes 786440 | tf_op jit(solution)/shard_map/ppermute | solution.py:212
  63.8 0.8 copy-start.2
  71.4 1.7 %copy-start.1 = (bf16[4,24,128,128]{3,2,1,0:T(8,128)(2,1)}, bf16[4,24,128,128]{3,2,1,0:T(8,128)(2,1)S(1)}, u32[]{:S(2)}) copy-start(bf16[4,24,128,128]{3,2,1,0:T(8,128)(2,1)S(1)} %get-tuple-element.14.tiles) | copy-start | bytes 9437188
  73.1 0.6 copy-start.4
  108.7 12.4 %copy-start.3 = (f32[4,256,128]{2,1,0:T(8,128)S(1)}, f32[4,256,128]{2,1,0:T(8,128)}, u32[]{:S(2)}) copy-start(f32[4,256,128]{2,1,0:T(8,128)} %copy-done.2) | copy-start | bytes 1572868
  109.0 13.2 %collective-permute-start.5 = (bf16[4,256,128]{2,1,0:T(8,128)(2,1)S(1)}, bf16[4,256,128]{2,1,0:T(8,128)(2,1)S(1)}, u32[]{:S(2)}, u32[]{:S(2)}) collective-permute-start(bf16[4,256,128]{2,1,0:T(8,128)(2,1)S(1)} %fusion.2.parts), channel_id=1, source_target_pairs={{0,1},{1,0},{2,3},{3,2},{4,5},{5,4},{6,7},{7,6},{8,9},{9,8},{10,11... | collective-permute-start | bytes 786440 | tf_op jit(solution)/shard_map/ppermute | solution.py:212
Sparse Core Ops, SparseCore 0:
  9.4 75.7 all-gather.1
